TPU v7x, 128 devices: a whole 4x4x4 slice. The times are simulated.
128 devices in a mesh: dp: 16 (over x_lo, z, core), section: 8 (over y, x_hi).
Axes of the slice: x: 4 (x_hi: 2, x_lo: 2; x = x_hi * 2 + x_lo), y: 4, z: 4, core: 2. Of those that a mesh axis runs over, the one named last changes fastest.
Arguments:
- encoded: bfloat16 [16, 64, 2560], P('dp', 'section'), may hold values from -6 to 6
- source_len: int32 [16], replicated, may hold values from 16 to 64, as said below
- queries: bfloat16 [8, 16, 128, 8192], P('section', 'dp'), may hold values from -2.5 to 2.5
- saved_keys: bfloat16 [8, 16, 64, 8192], P('section', 'dp'), may hold values from -2.5 to 2.5
- saved_values: bfloat16 [8, 16, 64, 8192], P('section', 'dp'), may hold values from -6 to 6
- out_grad: bfloat16 [8, 16, 128, 8192], P('section', 'dp'), may hold values from -6 to 6
- key_weight: bfloat16 [8, 2560, 8192], P('section', None, 'dp'), may hold values from -0.0625 to 0.0625
- value_weight: bfloat16 [8, 2560, 8192], P('section', None, 'dp'), may hold values from -0.0625 to 0.0625
Outputs:
- encoder_grad: float32 [16, 64, 2560], P('dp', 'section')
- key_update: float32 [8, 2560, 8192], P('section', None, 'dp')
- value_update: float32 [8, 2560, 8192], P('section', None, 'dp')
Inputs may be any that keep to these rules, and one draw needn't show every extreme that they name: `source_len`: some sample has no padding.
All inputs are finite; a program needn't handle non-finite values.
Results may differ from a plain program's by a relative error of at most 0.0063.
Values may be sent and summed in bfloat16 or wider, within the bound.
No kernel may reach another device: no remote copies, remote signals or barrier semaphores. Data moves between devices by JAX's collectives and lax.ppermute only.
A program may use at most 128 MiB of HBM per device.

v0:
```python
import math

import jax
import jax.numpy as jnp
from jax import lax
from jax.sharding import PartitionSpec as P

D = 2560
HEAD = 128
SWEEPS = 5


LINEAR_COEFF = 3.4445
SQUARE_COEFF = -4.775
CUBIC_COEFF = 2.0315


def orthogonalize(gradient):
    norms = jnp.sqrt(jnp.sum(gradient * gradient, axis=(0, 2), keepdims=True)) + 1e-07
    current = gradient / norms
    for sweep in range(SWEEPS):
        gram = jnp.einsum("dhi,dhj->hij", current, current, precision=lax.Precision.HIGHEST)
        squared = jnp.einsum("hij,hjk->hik", gram, gram, precision=lax.Precision.HIGHEST)
        mixer = SQUARE_COEFF * gram + CUBIC_COEFF * squared
        current = LINEAR_COEFF * current + jnp.einsum(
            "dhi,hij->dhj", current, mixer, precision=lax.Precision.HIGHEST
        )
    return current * math.sqrt(D)


def attention_grads(query_part, key_part, value_part, grad_part, valid):
    samples, tgt_rows, width = query_part.shape
    src_rows = key_part.shape[1]
    heads = width // HEAD
    query_four = query_part.reshape(samples, tgt_rows, heads, HEAD)
    key_four = key_part.reshape(samples, src_rows, heads, HEAD)
    value_four = value_part.reshape(samples, src_rows, heads, HEAD)
    grad_four = grad_part.reshape(samples, tgt_rows, heads, HEAD)
    scale = 1.0 / math.sqrt(HEAD)
    scores = (
        jnp.einsum("bthe,bshe->bhts", query_four, key_four, preferred_element_type=jnp.float32)
        * scale
    )
    weights_raw = jnp.exp(scores) * valid[:, None, None, :]
    probs = weights_raw / jnp.sum(weights_raw, axis=-1, keepdims=True)
    probs_low = probs.astype(jnp.bfloat16)
    grad_values = jnp.einsum(
        "bhts,bthe->bshe", probs_low, grad_four, preferred_element_type=jnp.float32
    ).astype(jnp.bfloat16)
    grad_probs = jnp.einsum(
        "bthe,bshe->bhts", grad_four, value_four, preferred_element_type=jnp.float32
    )
    delta = jnp.sum(probs * grad_probs, axis=-1, keepdims=True)
    grad_scores = (probs * (grad_probs - delta) * scale).astype(jnp.bfloat16)
    grad_keys = jnp.einsum(
        "bhts,bthe->bshe", grad_scores, query_four, preferred_element_type=jnp.float32
    ).astype(jnp.bfloat16)
    return (
        grad_keys.reshape(samples, src_rows, width),
        grad_values.reshape(samples, src_rows, width),
    )


def body(
    encoded, source_len, queries, saved_keys, saved_values, out_grad, key_weight, value_weight
):
    sections = lax.axis_size("section")
    src_rows = saved_keys.shape[2]
    own_len = lax.dynamic_slice_in_dim(source_len, lax.axis_index("dp"), 1, 0)
    own_valid = (jnp.arange(src_rows, dtype=jnp.int32)[None, :] < own_len[:, None]).astype(
        jnp.float32
    )
    local_keys, local_values = attention_grads(
        queries[0], saved_keys[0], saved_values[0], out_grad[0], own_valid
    )
    grad_keys, grad_values = (
        lax.all_to_all(local_keys, "dp", split_axis=2, concat_axis=0, tiled=True),
        lax.all_to_all(local_values, "dp", split_axis=2, concat_axis=0, tiled=True),
    )
    samples = grad_keys.shape[0]
    inner = grad_keys.shape[2]
    heads = inner // HEAD
    key_rows = grad_keys.reshape(samples * src_rows, inner)
    value_rows = grad_values.reshape(samples * src_rows, inner)
    layer_kw = key_weight[0]
    layer_vw = value_weight[0]
    width = layer_kw.shape[0]
    sample_rows = lax.all_gather(encoded, "section", axis=1, tiled=True)
    flat_rows = sample_rows.reshape(src_rows, width)
    piece = lax.all_gather(flat_rows, "dp", axis=0, tiled=True)
    key_sum = jnp.einsum("rd,ri->di", piece, key_rows, preferred_element_type=jnp.float32)
    value_sum = jnp.einsum("rd,ri->di", piece, value_rows, preferred_element_type=jnp.float32)
    block = src_rows // sections
    middle = lax.psum_scatter(
        jnp.einsum("ri,di->rd", key_rows, layer_kw, preferred_element_type=jnp.float32)
        + jnp.einsum("ri,di->rd", value_rows, layer_vw, preferred_element_type=jnp.float32),
        "dp",
        scatter_dimension=0,
        tiled=True,
    )
    owned = lax.psum_scatter(middle, "section", scatter_dimension=0, tiled=True)
    encoder_grad = owned.reshape(1, block, width)
    stacked = jnp.concatenate(
        [key_sum.reshape(width, heads, HEAD), value_sum.reshape(width, heads, HEAD)], axis=1
    )
    result = orthogonalize(stacked)
    key_update = result[:, :heads].reshape(1, width, inner)
    value_update = result[:, heads:].reshape(1, width, inner)
    return (encoder_grad, key_update, value_update)


def solution(mesh):
    in_specs = (
        P("dp", "section", None),
        P(),
        P("section", "dp", None, None),
        P("section", "dp", None, None),
        P("section", "dp", None, None),
        P("section", "dp", None, None),
        P("section", None, "dp"),
        P("section", None, "dp"),
    )
    out_specs = (P("dp", "section", None), P("section", None, "dp"), P("section", None, "dp"))
    return jax.shard_map(body, mesh=mesh, in_specs=in_specs, out_specs=out_specs, check_vma=False)
```

profile of v0, /device:TPU:0, one launch (start us, length us, event | category | flops | bytes accessed | tf_op | source)
XLA Modules:
  0.0 502.0 jit_solution(12664699753201054769)
XLA Ops:
  7.2 37.6 %all_gather.6 = bf16[1,64,2560]{2,1,0:T(8,128)(2,1)} all-gather(bf16[1,8,2560]{2,1,0:T(8,128)(2,1)} %param.8), channel_id=1, replica_groups=mesh['dp'=16,'section'=8] {'section'}, dimensions={1}, use_global_device_ids=true | all-gather | bytes 368640 | tf_op jit(solution)/shard_map/all_gather | solution.py:88
  55.8 5.6 %fusion.15 = f32[64,128,64]{1,2,0:T(8,128)} fusion(bf16[128,64,128]{2,1,0:T(8,128)(2,1)} %bitcast.136, bf16[64,64,128]{2,1,0:T(8,128)(2,1)} %bitcast.140), kind=kOutput, calls=%fused_computation.24 | convolution fusion | flops 134217728 | bytes 5242880 | tf_op jit(solution)/shard_map/bthe,bshe->bhts/dot_general | solution.py:50
  65.5 7.9 %fusion.36 = bf16[1,64,64,128]{3,1,2,0:T(8,128)(2,1)} fusion(bf16[128,64,128]{2,1,0:T(8,128)(2,1)} %bitcast.147, f32[64,128,64]{1,2,0:T(8,128)} %fusion.15, f32[64,128,64]{1,2,0:T(8,128)} %get-tuple-element.18, f32[64,128]{1,0:T(8,128)S(1)} %get-tuple-element.17, f32[64]{0:T(128)S(1)} %compare_convert_fusion), kind=kOutput, calls=%fused_computation.35 | convolution fusion | flops 140517440 | bytes 7373056 | tf_op jit(solution)/shard_map/bhts,bthe->bshe/dot_general | solution.py:55
  76.7 12.5 %reshape.122 = bf16[1,64,8192]{1,0,2:T(2,128)(2,1)} reshape(bf16[1,64,64,128]{1,3,2,0:T(8,128)(2,1)} %copy.134) | data formatting | bytes 2097152 | tf_op jit(solution)/shard_map/reshape | solution.py:59
  89.7 46.5 %reduce.4 = bf16[8192,64]{1,0:T(8,128)(2,1)} reduce(bf16[8192,1,64]{2,1,0:T(2,128)(2,1)} %bitcast.132, bf16[]{:T(256)} %broadcast.76), dimensions={1}, to_apply=%bitcast.85.reduce_sub_computation | reduce | bytes 2097154
  136.3 4.6 reshape.124
  140.9 7.0 %all-to-all-start = ((bf16[16,2,16384]{2,1,0:T(2,128)(2,1)}), bf16[16,2,16384]{2,1,0:T(2,128)(2,1)}, u32[]{:S(2)}, u32[]{:S(2)}) async-start(bf16[16,2,16384]{2,1,0:T(2,128)(2,1)} %reshape.124), calls=%async_computation | async-start | bytes 2097152 | tf_op jit(solution)/shard_map/all_to_all | solution.py:77
  147.9 5.4 %fusion.33 = bf16[1,64,64,128]{3,1,2,0:T(8,128)(2,1)} fusion(bf16[128,64,128]{2,1,0:T(8,128)(2,1)} %bitcast.137, f32[64,128,64]{1,2,0:T(8,128)} %get-tuple-element.18, f32[64,128]{1,0:T(8,128)S(1)} %get-tuple-element.17, f32[64]{0:T(128)S(1)} %compare_convert_fusion), kind=kOutput, calls=%fused_computation.34 | convolution fusion | flops 136839168 | bytes 5275904 | tf_op jit(solution)/shard_map/bhts,bthe->bshe/dot_general | solution.py:47
  156.1 12.5 %reshape.123 = bf16[1,64,8192]{1,0,2:T(2,128)(2,1)} reshape(bf16[1,64,64,128]{1,3,2,0:T(8,128)(2,1)} %copy.135) | data formatting | bytes 2097152 | tf_op jit(solution)/shard_map/reshape | solution.py:60
  168.6 46.5 %reduce.5 = bf16[8192,64]{1,0:T(8,128)(2,1)} reduce(bf16[8192,1,64]{2,1,0:T(2,128)(2,1)} %bitcast.133, bf16[]{:T(256)} %broadcast.76), dimensions={1}, to_apply=%bitcast.87.reduce_sub_computation | reduce | bytes 2097154
  215.1 4.6 reshape.126
  219.7 5.9 %all-to-all-start.1 = ((bf16[16,2,16384]{2,1,0:T(2,128)(2,1)}), bf16[16,2,16384]{2,1,0:T(2,128)(2,1)}, u32[]{:S(2)}, u32[]{:S(2)}) async-start(bf16[16,2,16384]{2,1,0:T(2,128)(2,1)} %reshape.126), calls=%async_computation.1 | async-start | bytes 2097152 | tf_op jit(solution)/shard_map/all_to_all | solution.py:78
  225.7 10.4 %reshape.125 = bf16[8192,1,64]{2,1,0:T(2,128)(2,1)} reshape(bf16[16,2,16384]{2,1,0:T(2,128)(2,1)} %all-to-all-done) | data formatting | bytes 2097152
  236.0 8.9 %copy.95 = bf16[1,64,8192]{2,1,0:T(8,128)(2,1)} copy(bf16[1,64,8192]{1,0,2:T(2,128)(2,1)} %bitcast.130) | data formatting | bytes 2097152 | tf_op jit(solution)/shard_map/all_to_all | solution.py:77
  248.1 10.2 %reshape.127 = bf16[8192,1,64]{2,1,0:T(2,128)(2,1)} reshape(bf16[16,2,16384]{2,1,0:T(2,128)(2,1)} %all-to-all-done.1) | data formatting | bytes 2097152
  258.3 8.9 %copy.100 = bf16[1,64,8192]{2,1,0:T(8,128)(2,1)} copy(bf16[1,64,8192]{1,0,2:T(2,128)(2,1)} %bitcast.131) | data formatting | bytes 2097152 | tf_op jit(solution)/shard_map/all_to_all | solution.py:78
  272.5 5.5 %convolution_add_fusion = f32[1024,2560]{1,0:T(8,128)} fusion(f32[1024,2560]{1,0:T(8,128)S(1)} %fusion.8, bf16[1024,512]{1,0:T(8,128)(2,1)S(1)} %bitcast.134, bf16[1,2560,512]{2,1,0:T(8,128)(2,1)S(1)} %copy-done.9), kind=kOutput, calls=%fused_computation.10 | convolution fusion | flops 2686976000 | bytes 24641536 | tf_op jit(solution)/shard_map/ri,di->rd/dot_general | solution.py:96
  279.2 5.5 %fusion.3 = f32[512,2560]{1,0:T(8,128)S(1)} fusion(bf16[1024,512]{1,0:T(8,128)(2,1)S(1)} %bitcast.135, bf16[1,1024,2560]{2,1,0:T(8,128)(2,1)} %all-gather.3.cloned.1.call-done), kind=kOutput, calls=%fused_computation.11 | convolution fusion | flops 2684354560 | bytes 11534336 | tf_op jit(solution)/shard_map/rd,ri->di/dot_general | solution.py:92
  290.1 10.6 %fusion.52 = f32[8,128,128]{2,1,0:T(8,128)S(1)} fusion(f32[2560,4,128]{0,2,1:T(8,128)S(1)} %bitcast.125, f32[2560,4,128]{0,2,1:T(8,128)S(1)} %bitcast.128, f32[8]{0:T(128)S(1)} %sqrt_add_fusion), kind=kOutput, calls=%fused_computation.56 | convolution fusion | flops 4031774720 | bytes 11010080 | tf_op jit(solution)/shard_map/dhi,dhj->hij/dot_general | solution.py:22
  301.4 15.0 %bitcast_add_fusion.4 = f32[2560,8,128]{0,2,1:T(8,128)} fusion(f32[8,128,128]{2,1,0:T(8,128)S(1)} %fusion.45, f32[8]{0:T(128)S(1)} %sqrt_add_fusion, f32[2560,4,128]{0,2,1:T(8,128)S(1)} %bitcast.126, f32[2560,4,128]{0,2,1:T(8,128)} %bitcast.129), kind=kOutput, calls=%fused_computation.7 | convolution fusion | flops 4042260480 | bytes 21495840 | tf_op jit(solution)/shard_map/dhi,hij->dhj/dot_general | solution.py:25
  316.4 17.0 %fusion.59 = f32[8,128,128]{2,1,0:T(8,128)S(1)} fusion(f32[2560,8,128]{0,2,1:T(8,128)} %bitcast_add_fusion.4), kind=kOutput, calls=%fused_computation.58 | convolution fusion | flops 4026531840 | bytes 11010048 | tf_op jit(solution)/shard_map/dhi,dhj->hij/dot_general | solution.py:22
  334.1 19.0 %bitcast_add_fusion.3 = f32[2560,8,128]{0,2,1:T(8,128)S(1)} fusion(f32[2560,8,128]{0,2,1:T(8,128)} %bitcast_add_fusion.4, f32[8,128,128]{2,1,0:T(8,128)S(1)} %fusion.44), kind=kOutput, calls=%fused_computation.6 | convolution fusion | flops 4031774720 | bytes 21495808 | tf_op jit(solution)/shard_map/dhi,hij->dhj/dot_general | solution.py:25
  353.1 9.6 %fusion.60 = f32[8,128,128]{2,1,0:T(8,128)S(1)} fusion(f32[2560,8,128]{0,2,1:T(8,128)S(1)} %bitcast_add_fusion.3), kind=kOutput, calls=%fused_computation.59 | convolution fusion | flops 4026531840 | bytes 11010048 | tf_op jit(solution)/shard_map/dhi,dhj->hij/dot_general | solution.py:22
  363.4 13.5 %bitcast_add_fusion.2 = f32[2560,8,128]{0,2,1:T(8,128)} fusion(f32[2560,8,128]{0,2,1:T(8,128)S(1)} %bitcast_add_fusion.3, f32[8,128,128]{2,1,0:T(8,128)S(1)} %fusion.43), kind=kOutput, calls=%fused_computation.5 | convolution fusion | flops 4031774720 | bytes 21495808 | tf_op jit(solution)/shard_map/dhi,hij->dhj/dot_general | solution.py:25
  376.9 16.8 %fusion.61 = f32[8,128,128]{2,1,0:T(8,128)S(1)} fusion(f32[2560,8,128]{0,2,1:T(8,128)} %bitcast_add_fusion.2), kind=kOutput, calls=%fused_computation.60 | convolution fusion | flops 4026531840 | bytes 11010048 | tf_op jit(solution)/shard_map/dhi,dhj->hij/dot_general | solution.py:22
  394.4 18.7 %bitcast_add_fusion.1 = f32[2560,8,128]{0,2,1:T(8,128)S(1)} fusion(f32[2560,8,128]{0,2,1:T(8,128)} %bitcast_add_fusion.2, f32[8,128,128]{2,1,0:T(8,128)S(1)} %fusion.42), kind=kOutput, calls=%fused_computation.4 | convolution fusion | flops 4031774720 | bytes 21495808 | tf_op jit(solution)/shard_map/dhi,hij->dhj/dot_general | solution.py:25
  413.1 9.6 %fusion.62 = f32[8,128,128]{2,1,0:T(8,128)S(1)} fusion(f32[2560,8,128]{0,2,1:T(8,128)S(1)} %bitcast_add_fusion.1), kind=kOutput, calls=%fused_computation.61 | convolution fusion | flops 4026531840 | bytes 11010048 | tf_op jit(solution)/shard_map/dhi,dhj->hij/dot_general | solution.py:22
  423.4 17.9 %fusion.1 = f32[2560,8,128]{0,2,1:T(8,128)S(1)} fusion(f32[2560,8,128]{0,2,1:T(8,128)} %copy-done.2, f32[8,128,128]{2,1,0:T(8,128)S(1)} %fusion.41), kind=kOutput, calls=%fused_computation.3 | convolution fusion | flops 4034396160 | bytes 21495808 | tf_op jit(solution)/shard_map/dhi,hij->dhj/dot_general | solution.py:25
  441.3 5.3 %fusion.58 = (f32[2560,4,128]{0,2,1:T(8,128)}, f32[2560,4,128]{0,2,1:T(8,128)}) fusion(f32[2560,8,128]{0,2,1:T(8,128)S(1)} %fusion.1), kind=kLoop, calls=%fused_computation.57 | loop fusion | bytes 20971520 | tf_op jit(solution)/shard_map/slice | solution.py:108
  446.6 5.9 %copy.117 = f32[1,2560,512]{2,1,0:T(8,128)} copy(f32[1,2560,512]{1,2,0:T(8,128)} %bitcast.123) | data formatting | bytes 10485760
  452.5 6.0 %copy.118 = f32[1,2560,512]{2,1,0:T(8,128)} copy(f32[1,2560,512]{1,2,0:T(8,128)} %bitcast.122) | data formatting | bytes 10485760
  458.6 36.4 %reduce-scatter.5.cloned.1.call-done = f32[8,2560]{1,0:T(8,128)} async-done(((f32[64,2560]{1,0:T(8,128)}), f32[8,2560]{1,0:T(8,128)}) %reduce-scatter.5.cloned.1.call-update) | async-done | bytes 81936 | tf_op jit(solution)/shard_map/reduce_scatter | solution.py:101
  (65 shorter events, 40.0 us)
Async XLA Ops:
  7.2 262.3 %copy-start = (bf16[1,2560,512]{2,1,0:T(8,128)(2,1)S(1)}, bf16[1,2560,512]{2,1,0:T(8,128)(2,1)}, u32[]{:S(2)}) copy-start(bf16[1,2560,512]{2,1,0:T(8,128)(2,1)} %param.14) | copy-start | bytes 7864324
  7.2 270.9 %all-gather.3.cloned.1.call-start = ((), (), s32[]{:S(2)}) async-start(), calls=%async_computation.6 | async-start | bytes 5570560 | tf_op jit(solution)/shard_map/all_gather | solution.py:90
  44.9 3.7 copy-start.10
  44.9 5.6 %copy-start.12 = (bf16[1,1,64,8192]{3,2,1,0:T(8,128)(2,1)S(1)}, bf16[1,1,64,8192]{3,2,1,0:T(8,128)(2,1)}, u32[]{:S(2)}) copy-start(bf16[1,1,64,8192]{3,2,1,0:T(8,128)(2,1)} %param.12) | copy-start | bytes 3145732
  48.6 5.7 %copy-start.14 = (s32[16]{0:T(128)S(1)}, s32[16]{0:T(128)}, u32[]{:S(2)}) copy-start(s32[16]{0:T(128)} %param.9) | copy-start | bytes 196
  54.3 7.1 %copy-start.11 = (bf16[16,8,64,128]{3,2,1,0:T(8,128)(2,1)S(1)}, bf16[16,8,64,128]{3,2,1,0:T(8,128)(2,1)}, u32[]{:S(2)}) copy-start(bf16[16,8,64,128]{3,2,1,0:T(8,128)(2,1)} %copy.138) | copy-start | bytes 6291460
  54.3 7.1 %copy-start.13 = (bf16[8,8,64,128]{3,2,1,0:T(8,128)(2,1)S(1)}, bf16[8,8,64,128]{3,2,1,0:T(8,128)(2,1)}, u32[]{:S(2)}) copy-start(bf16[8,8,64,128]{3,2,1,0:T(8,128)(2,1)} %copy.139) | copy-start | bytes 3145732
  140.9 78.8 %all-to-all-start = ((bf16[16,2,16384]{2,1,0:T(2,128)(2,1)}), bf16[16,2,16384]{2,1,0:T(2,128)(2,1)}, u32[]{:S(2)}, u32[]{:S(2)}) async-start(bf16[16,2,16384]{2,1,0:T(2,128)(2,1)} %reshape.124), calls=%async_computation | async-start | bytes 2097152 | tf_op jit(solution)/shard_map/all_to_all | solution.py:77
  219.7 28.4 %all-to-all-start.1 = ((bf16[16,2,16384]{2,1,0:T(2,128)(2,1)}), bf16[16,2,16384]{2,1,0:T(2,128)(2,1)}, u32[]{:S(2)}, u32[]{:S(2)}) async-start(bf16[16,2,16384]{2,1,0:T(2,128)(2,1)} %reshape.126), calls=%async_computation.1 | async-start | bytes 2097152 | tf_op jit(solution)/shard_map/all_to_all | solution.py:78
  225.6 197.8 %reduce-scatter.3.cloned.1.call-start = ((), (), s32[]{:S(2)}) async-start(), calls=%async_computation.4 | async-start | bytes 11141120 | tf_op jit(solution)/shard_map/reduce_scatter | solution.py:94
  267.2 2.4 copy-start.7
  269.5 3.0 copy-start.5
  269.5 3.0 copy-start.9
  278.0 1.2 copy-start.6
  278.0 6.7 %copy-start.8 = (bf16[16,1,64,512]{3,2,0,1:T(8,128)(2,1)S(1)}, bf16[16,1,64,512]{3,2,0,1:T(8,128)(2,1)}, u32[]{:S(2)}) copy-start(bf16[16,1,64,512]{3,2,0,1:T(8,128)(2,1)} %copy.96) | copy-start | bytes 3145732
  278.1 216.9 %reduce-scatter.5.cloned.1.call-start = ((), (), s32[]{:S(2)}) async-start(), calls=%async_computation.5 | async-start | bytes 737280 | tf_op jit(solution)/shard_map/reduce_scatter | solution.py:101
  279.2 5.5 %copy-start.3 = (bf16[1,1024,2560]{2,1,0:T(8,128)(2,1)S(1)}, bf16[1,1024,2560]{2,1,0:T(8,128)(2,1)}, u32[]{:S(2)}) copy-start(bf16[1,1024,2560]{2,1,0:T(8,128)(2,1)} %all-gather.3.cloned.1.call-done) | copy-start | bytes 15728644
  287.8 2.4 copy-start.4
  413.1 9.6 %copy-start.2 = (f32[2560,8,128]{0,2,1:T(8,128)}, f32[2560,8,128]{0,2,1:T(8,128)S(1)}, u32[]{:S(2)}) copy-start(f32[2560,8,128]{0,2,1:T(8,128)S(1)} %bitcast_add_fusion.1) | copy-start | bytes 31457284
  452.5 42.5 %copy-start.1 = (bf16[1,2560,512]{2,1,0:T(8,128)(2,1)S(1)}, bf16[1,2560,512]{2,1,0:T(8,128)(2,1)}, u32[]{:S(2)}) copy-start(bf16[1,2560,512]{2,1,0:T(8,128)(2,1)} %param.14) | copy-start | bytes 7864324
Sparse Core Ops, SparseCore 0:
  45.0 41.5 all-gather.2
  278.2 79.5 reduce-scatter.2
  423.5 71.4 reduce-scatter.4
where the time goes:
time: 512 us; the launch traced here: 502 us
  matrix products  191 us (37%)
  local copies, waits for them, and re-layouts  114 us (22%)
  other arithmetic  94.9 us (19%)
  blocking collectives  37.6 us (7%)
  waiting for transfers between devices  36.5 us (7%)
  between operations  14.5 us (3%)
  starting transfers between devices  13 us (3%)
    unnamed x2, other arithmetic  93.1 us
    dot_general x5, matrix products, orthogonalize(): jnp.einsum('dhi,hij->dhj', current, mixer, precision=lax.Precision.HIGHEST)  84.1 us
    dot_general x5, matrix products, orthogonalize(): jnp.einsum('dhi,dhj->hij', current, current, precision=lax.Precision.HIGH...  63.7 us
    unnamed x43, local copies, waits for them, and re-layouts  57.5 us
    all_gather x1, blocking collectives, body(): sample_rows = lax.all_gather(encoded, 'section', axis=1, tiled=True)  37.6 us
    reduce_scatter x1, waiting for transfers between devices, body(): owned = lax.psum_scatter(middle, 'section', scatter_dimension=0, tiled=True)  36.4 us
    reshape x2, local copies, waits for them, and re-layouts, attention_grads(): grad_keys.reshape(samples, src_rows, width)  15.8 us
    reshape x2, local copies, waits for them, and re-layouts, attention_grads(): grad_values.reshape(samples, src_rows, width)  15.2 us
  transfers between devices with their start and end apart: 5, of which 1 were waited for; matrix products, arithmetic and copies ran while one was open for 79% of the time, Pallas kernels for 0%

commit v1 on v0

v1 whole, which is shorter than its diff:
```python
import functools
import math

import jax
import jax.numpy as jnp
from jax import lax
from jax.experimental import pallas as pl
from jax.experimental.pallas import tpu as pltpu
from jax.sharding import Mesh, PartitionSpec as P

D = 2560
HEAD = 128
SWEEPS = 5

LINEAR_COEFF = 3.4445
SQUARE_COEFF = -4.775
CUBIC_COEFF = 2.0315

BF16 = jnp.bfloat16
F32 = jnp.float32
HIGHEST = lax.Precision.HIGHEST

MIB = 1024 * 1024


def dot(a, b, dims, precision=None):
    return lax.dot_general(a, b, (dims, ((), ())), precision=precision, preferred_element_type=F32)


def attention_kernel(place, lens, q_ref, k_ref, v_ref, g_ref, out_ref):
    src = k_ref.shape[0]
    tgt = q_ref.shape[0]
    heads = q_ref.shape[1] // HEAD
    row = lax.broadcasted_iota(jnp.int32, (src, tgt), 0)
    valid = (row < lens[place[0]]).astype(F32)
    scale = 1.0 / math.sqrt(HEAD)
    width = heads * HEAD
    cols = [slice(h * HEAD, (h + 1) * HEAD) for h in range(heads)]
    cat = jnp.concatenate
    both = [
        dot(cat([k_ref[:, c], v_ref[:, c]], 0), cat([q_ref[:, c], g_ref[:, c]], 0), ((1,), (1,))) for c in cols
    ]
    grad_probs = [b[src:, tgt:] for b in both]
    raw = [jnp.exp2(b[:src, :tgt] * (scale * math.log2(math.e))) * valid for b in both]
    probs = [r * (1.0 / jnp.sum(r, axis=0, keepdims=True)) for r in raw]
    delta = [jnp.sum(p * g, axis=0, keepdims=True) for p, g in zip(probs, grad_probs)]
    low = [
        cat([(p * ((g - d) * scale)).astype(BF16), p.astype(BF16)], 0)
        for p, g, d in zip(probs, grad_probs, delta)
    ]
    for h, c in enumerate(cols):
        grads = dot(low[h], cat([q_ref[:, c], g_ref[:, c]], 1), ((1,), (0,)))
        out_ref[:, c] = grads[:src, :HEAD].astype(BF16)
        out_ref[:, width + h * HEAD : width + (h + 1) * HEAD] = grads[src:, HEAD:].astype(BF16)


def attention(place, lens, q, k, v, g, chips, group):
    tgt, src = q.shape[0], k.shape[0]

    def col(p, r, place, lens):
        return (0, 2 * p + lax.bitwise_xor(lax.rem(place[0], 2), r))

    return pl.pallas_call(
        attention_kernel,
        grid_spec=pltpu.PrefetchScalarGridSpec(
            num_scalar_prefetch=2,
            grid=(chips, 2),
            in_specs=[
                pl.BlockSpec((tgt, group), col),
                pl.BlockSpec((src, group), col),
                pl.BlockSpec((src, group), col),
                pl.BlockSpec((tgt, group), col),
            ],
            out_specs=pl.BlockSpec((None, src, 2 * group), lambda p, r, place, lens: (p, 0, r)),
        ),
        out_shape=jax.ShapeDtypeStruct((chips, src, 4 * group), BF16),
        compiler_params=pltpu.CompilerParams(vmem_limit_bytes=56 * MIB),
        cost_estimate=pl.CostEstimate(flops=700_000_000, bytes_accessed=8 * MIB, transcendentals=600_000),
        name="attention",
    )(place, lens, q, k, v, g)


def partial_kernel(kv_ref, kw_ref, vw_ref, okw_ref, ovw_ref, out_ref):
    w = kw_ref.shape[1]
    total = None
    for i, ref in enumerate((kw_ref, vw_ref, okw_ref, ovw_ref)):
        term = dot(kv_ref[:, i * w : (i + 1) * w], ref[...], ((1,), (1,)))
        total = term if total is None else total + term
    out_ref[...] = total.astype(BF16)


def encoder_partial(kv, kw, vw, okw, ovw):
    rows, feats = kv.shape
    width, w = kw.shape
    tile = 512
    spec = pl.BlockSpec((tile, w), lambda j: (j, 0))
    return pl.pallas_call(
        partial_kernel,
        grid=(width // tile,),
        in_specs=[pl.BlockSpec((rows, feats), lambda j: (0, 0)), spec, spec, spec, spec],
        out_specs=pl.BlockSpec((rows, tile), lambda j: (0, j)),
        out_shape=jax.ShapeDtypeStruct((rows, width), BF16),
        compiler_params=pltpu.CompilerParams(vmem_limit_bytes=56 * MIB),
        cost_estimate=pl.CostEstimate(
            flops=2 * rows * feats * width, bytes_accessed=16 * MIB, transcendentals=0
        ),
        name="encoder_partial",
    )(kv, kw, vw, okw, ovw)


def two_parts(x):
    high = x.astype(BF16)
    low = (x - high.astype(F32)).astype(BF16)
    return high, low


def update_kernel(pairs, e_ref, oe_ref, kv_ref, okv_ref, key_ref, value_ref, parts, gram, mix):
    step = pl.program_id(0)
    width = e_ref.shape[1]
    heads = 2 * pairs

    @pl.when(step < pairs)
    def _():
        total = dot(kv_ref[...], e_ref[...], ((0,), (0,))) + dot(okv_ref[...], oe_ref[...], ((0,), (0,)))
        for h in range(2):
            high, low = two_parts(total[h * HEAD : (h + 1) * HEAD])
            both = jnp.concatenate([high, low], axis=0)
            parts[2 * step + h] = both
            full = dot(both, both, ((1,), (1,)))
            gram[2 * step + h] = (full[:HEAD, :HEAD] + full[HEAD:, HEAD:]) + (
                full[:HEAD, HEAD:] + full[HEAD:, :HEAD]
            )

    @pl.when(step == pairs)
    def _():
        row = lax.broadcasted_iota(jnp.int32, (HEAD, HEAD), 0)
        eye = (row == lax.broadcasted_iota(jnp.int32, (HEAD, HEAD), 1)).astype(F32)

        def prod(a, b):
            return dot(a, b, ((1,), (0,)), HIGHEST)

        for h in range(heads):
            whole = gram[h]
            trace = jnp.sum(jnp.sum(whole * eye, axis=1, keepdims=True), axis=0, keepdims=True)
            inverse = 1.0 / (jnp.sqrt(trace) + 1e-07)
            gram[h] = whole * inverse * inverse
            mix[h] = eye * (inverse * math.sqrt(width))

        def sweep(_, carry):
            grams = [gram[h] for h in range(heads)]
            squares = [prod(a, a) for a in grams]
            steps = [
                LINEAR_COEFF * eye + (SQUARE_COEFF * a + CUBIC_COEFF * s) for a, s in zip(grams, squares)
            ]
            halves = [prod(a, m) for a, m in zip(grams, steps)]
            mixes = [prod(mix[h], m) for h, m in enumerate(steps)]
            nexts = [prod(m, a) for a, m in zip(halves, steps)]
            for h in range(heads):
                gram[h] = nexts[h]
                mix[h] = mixes[h]
            return carry

        lax.fori_loop(0, SWEEPS, sweep, 0)

    def finish(ref):
        first = 2 * (step - pairs - 1)
        for h in range(2):
            high, low = two_parts(mix[first + h])
            line = jnp.concatenate([high, low], axis=1)
            right = jnp.concatenate([line, line], axis=0)
            out = dot(parts[first + h], right, ((0,), (0,)))
            ref[:, h * HEAD : (h + 1) * HEAD] = out[:, :HEAD] + out[:, HEAD:]

    @pl.when(jnp.logical_and(step > pairs, step <= pairs + pairs // 2))
    def _():
        finish(key_ref)

    @pl.when(step > pairs + pairs // 2)
    def _():
        finish(value_ref)


def updates(e, oe, kv, okv, inner):
    rows, width = e.shape
    heads = 2 * inner // HEAD
    pairs = heads // 2
    half = pairs // 2
    wide = 2 * HEAD
    whole = pl.BlockSpec((rows, width), lambda i: (0, 0))
    cols = pl.BlockSpec((rows, wide), lambda i: (0, jnp.minimum(i, pairs - 1)))
    return pl.pallas_call(
        functools.partial(update_kernel, pairs),
        grid=(2 * pairs + 1,),
        in_specs=[whole, whole, cols, cols],
        out_specs=[
            pl.BlockSpec((width, wide), lambda i: (0, jnp.clip(i - pairs - 1, 0, half - 1))),
            pl.BlockSpec((width, wide), lambda i: (0, jnp.clip(i - pairs - 1 - half, 0, half - 1))),
        ],
        out_shape=[jax.ShapeDtypeStruct((width, inner), F32)] * 2,
        scratch_shapes=[
            pltpu.VMEM((heads, 2 * HEAD, width), BF16),
            pltpu.VMEM((heads, HEAD, HEAD), F32),
            pltpu.VMEM((heads, HEAD, HEAD), F32),
        ],
        compiler_params=pltpu.CompilerParams(vmem_limit_bytes=56 * MIB),
        cost_estimate=pl.CostEstimate(
            flops=20_000_000_000, bytes_accessed=20 * MIB, transcendentals=0
        ),
        name="updates",
    )(e, oe, kv, okv)


def ring(size, shift):
    return [(j, (j + shift) % size) for j in range(size)]


def gather_ring(block, axis, size, dim):
    own = lax.axis_index(axis)
    got = [(0, block)]
    for shift in ((2, 1, 3) if size == 4 else range(1, size)):
        got.append((shift, lax.ppermute(block, axis, ring(size, shift))))
    shape = block.shape[:dim] + (size,) + block.shape[dim:]
    out = jnp.zeros(shape, block.dtype)
    for shift, piece in got:
        out = lax.dynamic_update_index_in_dim(out, piece, lax.rem(own - shift + size, size), dim)
    return out


def body(
    encoded, source_len, queries, saved_keys, saved_values, out_grad, key_weight, value_weight
):
    across = [(0, 1), (1, 0)]
    key_weight, value_weight = key_weight[0], value_weight[0]
    width, inner = key_weight.shape
    block = encoded.shape[1]

    spread = jnp.broadcast_to(encoded, (16, block, width))
    near = lax.all_to_all(spread, ("xl", "z", "xh"), split_axis=0, concat_axis=0, tiled=True)

    place = lax.axis_index(("xl", "z", "c")).astype(jnp.int32).reshape(1)
    local = attention(
        place, source_len, queries[0, 0], saved_keys[0, 0], saved_values[0, 0], out_grad[0, 0], 8, inner
    )
    moved = lax.all_to_all(local, ("xl", "z"), split_axis=0, concat_axis=0, tiled=True)
    rows = moved.reshape(8 * local.shape[1], 4 * inner)

    near, key_send, value_send, _ = lax.optimization_barrier((near, key_weight, value_weight, local))
    own_rows = gather_ring(near.reshape(8, 2 * block, width), "y", 4, 1).reshape(64 * block, width)
    other_kw = lax.ppermute(key_send, "c", across)
    other_vw = lax.ppermute(value_send, "c", across)
    other_rows = lax.ppermute(own_rows, "c", across)

    partial = encoder_partial(rows, key_weight, value_weight, other_kw, other_vw)
    terms = lax.all_to_all(partial, ("xl", "z", "y", "xh"), split_axis=0, concat_axis=0, tiled=True)
    held, _ = lax.optimization_barrier((rows, partial))
    other_kv = lax.ppermute(held[:, 2 * inner :], "c", across)
    key_update, value_update = updates(own_rows, other_rows, held, other_kv, inner)
    encoder_grad = jnp.sum(terms.reshape(64, block, width).astype(F32), axis=0)
    return encoder_grad[None], key_update[None], value_update[None]


def solution(mesh):
    fine = Mesh(mesh.devices.reshape(2, 4, 2, 4, 2), ("xl", "z", "c", "y", "xh"))
    dp, section = ("xl", "z", "c"), ("y", "xh")
    in_specs = (
        P(dp, section, None),
        P(),
        P(section, dp, None, None),
        P(section, dp, None, None),
        P(section, dp, None, None),
        P(section, dp, None, None),
        P(section, None, dp),
        P(section, None, dp),
    )
    out_specs = (P(dp, section, None), P(section, None, dp), P(section, None, dp))
    return jax.shard_map(body, mesh=fine, in_specs=in_specs, out_specs=out_specs, check_vma=False)
```

time: 512 us -> 120 us (0.23); the launches traced: 502 us -> 119 us
  matrix products: 191 us -> 0 us
  local copies, waits for them, and re-layouts: 114 us -> 10.6 us
  other arithmetic: 94.9 us -> 1.01 us
  Pallas kernels: 0 us -> 53.8 us
  blocking collectives: 37.6 us -> 0 us
  starting transfers between devices: 13 us -> 29.8 us
  between operations: 14.5 us -> 0.69 us
  waiting for transfers between devices: 36.5 us -> 23.2 us
    dot_general x23 -> x0, matrix products: 191 us -> none  [the longest x5 84.1 us: orthogonalize(): jnp.einsum('dhi,hij->dhj', current, mixer, precision=lax.Precision.HIGHEST)]
    unnamed x2 -> x0, other arithmetic: 93.1 us -> none
    unnamed x43 -> x2, local copies, waits for them, and re-layouts: 57.5 us -> 1.29 us
    pallas_call x0 -> x3, Pallas kernels: none -> 53.8 us  [the longest x1 28.8 us: updates(): pl.pallas_call(functools.partial(update_kernel, pairs), grid=(2 * pairs +...]
    all_gather x1 -> x0, blocking collectives: 37.6 us -> none  [body(): sample_rows = lax.all_gather(encoded, 'section', axis=1, tiled=True)]
    reduce_scatter x2 -> x0, waiting for transfers between devices: 36.4 us -> none  [the longest x1 36.4 us: body(): owned = lax.psum_scatter(middle, 'section', scatter_dimension=0, tiled=True)]
    reshape x4 -> x0, local copies, waits for them, and re-layouts: 31 us -> none  [the longest x2 15.8 us: attention_grads(): grad_keys.reshape(samples, src_rows, width)]
    all_to_all x6 -> x0, local copies, waits for them, and re-layouts: 20 us -> none  [the longest x3 10.5 us: body(): lax.all_to_all(local_keys, 'dp', split_axis=2, concat_axis=0, tiled=True)]
  transfers between devices with their start and end apart: 5 -> 10, of which waited for: 1 -> 4; matrix products, arithmetic and copies ran while one was open for 79% -> 6% of each run, Pallas kernels for 0% -> 45%
where the time goes in v1:
time: 120 us; the launch traced here: 119 us
  Pallas kernels  53.8 us (45%)
  starting transfers between devices  29.8 us (25%)
  waiting for transfers between devices  23.2 us (19%)
  local copies, waits for them, and re-layouts  10.6 us (9%)
    pallas_call x1, Pallas kernels, updates(): pl.pallas_call(functools.partial(update_kernel, pairs), grid=(2 * pairs +...  28.8 us
    ppermute x3, waiting for transfers between devices, gather_ring(): got.append((shift, lax.ppermute(block, axis, ring(size, shift))))  16.8 us
    pallas_call x1, Pallas kernels, attention(): pl.pallas_call(attention_kernel, grid_spec=pltpu.PrefetchScalarGridSpec(n...  14.3 us
    pallas_call x1, Pallas kernels, encoder_partial(): pl.pallas_call(partial_kernel, grid=(width // tile,), in_specs=[pl.BlockS...  10.8 us
    all_to_all x1, starting transfers between devices, body(): lax.all_to_all(partial, ('xl', 'z', 'y', 'xh'), split_axis=0, concat_axis...  10.5 us
    all_to_all x1, starting transfers between devices, body(): lax.all_to_all(spread, ('xl', 'z', 'xh'), split_axis=0, concat_axis=0, ti...  7.96 us
    all_to_all x1, waiting for transfers between devices, body(): lax.all_to_all(partial, ('xl', 'z', 'y', 'xh'), split_axis=0, concat_axis...  6.01 us
    all_to_all x1, starting transfers between devices, body(): lax.all_to_all(local, ('xl', 'z'), split_axis=0, concat_axis=0, tiled=True)  5.59 us
  transfers between devices with their start and end apart: 10, of which 4 were waited for; matrix products, arithmetic and copies ran while one was open for 6% of the time, Pallas kernels for 45%

profile of v1, /device:TPU:0, one launch (start us, length us, event | category | flops | bytes accessed | tf_op | source)
XLA Modules:
  0.0 119.2 jit_solution(17048833186160373839)
XLA Ops:
  0.6 1.7 %broadcast_in_dim.33 = bf16[16,8,2560]{2,1,0:T(8,128)(2,1)} broadcast(bf16[8,2560]{1,0:T(8,128)(2,1)} %bitcast.39), dimensions={1,2} | broadcast | bytes 696320 | tf_op jit(solution)/shard_map/broadcast_in_dim | solution.py:237
  2.3 8.0 %all-to-all-start.1 = ((bf16[16,8,2560]{2,1,0:T(8,128)(2,1)}), bf16[16,8,2560]{2,1,0:T(8,128)(2,1)S(1)}, u32[]{:S(2)}, u32[]{:S(2)}) async-start(bf16[16,8,2560]{2,1,0:T(8,128)(2,1)} %broadcast_in_dim.33), calls=%async_computation.1 | async-start | bytes 1310720 | tf_op jit(solution)/shard_map/all_to_all | solution.py:238
  10.3 14.3 %attention.1 = bf16[8,64,2048]{2,1,0:T(8,128)(2,1)} custom-call(s32[1]{0:T(128)} %bitcast.place, s32[16]{0:T(128)} %lens.1, bf16[128,8192]{1,0:T(8,128)(2,1)} %bitcast.34, bf16[64,8192]{1,0:T(8,128)(2,1)} %bitcast.36, bf16[64,8192]{1,0:T(8,128)(2,1)} %bitcast.37, bf16[128,8192]{1,0:T(8,128)(2,1)} %bitcast.35), custom_call_target="tpu_custom_call" | custom-call | flops 700000000 | bytes 8388608 | tf_op jit(solution)/shard_map/attention/pallas_call | solution.py:63
  24.6 0.0 all-to-all-done.1
  24.6 3.2 %collective-permute-start.2 = (bf16[8,16,2560]{2,1,0:T(8,128)(2,1)S(1)}, bf16[8,16,2560]{2,1,0:T(8,128)(2,1)S(1)}, u32[]{:S(2)}, u32[]{:S(2)}) collective-permute-start(bf16[8,16,2560]{2,1,0:T(8,128)(2,1)S(1)} %bitcast.30), channel_id=1, source_target_pairs={{0,4},{2,6},{4,0},{6,2},{1,5},{3,7},{5,1},{7,3},{8,12},{10,14},{12... | collective-permute-start | bytes 1966088 | tf_op jit(solution)/shard_map/ppermute | solution.py:221
  27.8 5.6 %all-to-all-start = ((bf16[8,64,2048]{2,1,0:T(8,128)(2,1)}), bf16[8,64,2048]{2,1,0:T(8,128)(2,1)S(1)}, u32[]{:S(2)}, u32[]{:S(2)}) async-start(bf16[8,64,2048]{2,1,0:T(8,128)(2,1)} %attention.1), calls=%async_computation | async-start | bytes 4194304 | tf_op jit(solution)/shard_map/all_to_all | solution.py:244
  33.3 1.1 collective-permute-start.4
  34.4 1.0 collective-permute-start.3
  35.4 0.0 collective-permute-start
  35.4 0.5 collective-permute-start.1
  35.9 1.8 %broadcast_in_dim.35 = bf16[8,4,16,2560]{3,2,1,0:T(8,128)(2,1)} broadcast(bf16[]{:T(256)} %constant.51.clone.1), dimensions={} | broadcast | bytes 2621442 | tf_op jit(solution)/shard_map/broadcast_in_dim | solution.py:223
  37.7 0.9 constant_dynamic-update-slice_fusion
  38.6 5.2 %collective-permute-done.2 = bf16[8,16,2560]{2,1,0:T(8,128)(2,1)S(1)} collective-permute-done((bf16[8,16,2560]{2,1,0:T(8,128)(2,1)S(1)}, bf16[8,16,2560]{2,1,0:T(8,128)(2,1)S(1)}, u32[]{:S(2)}, u32[]{:S(2)}) %collective-permute-start.2) | collective-permute-done | bytes 655392 | tf_op jit(solution)/shard_map/ppermute | solution.py:221
  43.8 0.9 bitcast_dynamic-update-slice_fusion.1
  44.7 11.6 %collective-permute-done.3 = bf16[8,16,2560]{2,1,0:T(8,128)(2,1)S(1)} collective-permute-done((bf16[8,16,2560]{2,1,0:T(8,128)(2,1)S(1)}, bf16[8,16,2560]{2,1,0:T(8,128)(2,1)S(1)}, u32[]{:S(2)}, u32[]{:S(2)}) %collective-permute-start.3) | collective-permute-done | bytes 655392 | tf_op jit(solution)/shard_map/ppermute | solution.py:221
  56.3 0.9 bitcast_dynamic-update-slice_fusion
  57.2 0.0 collective-permute-done.4
  57.2 0.9 bitcast_dynamic-update-slice_fusion.2
  58.1 0.0 collective-permute-start.5
  58.1 0.4 all-to-all-done
  58.5 0.0 collective-permute-done.okw_ref
  58.5 0.0 collective-permute-done.1.ovw_ref
  58.5 1.3 %copy-done = bf16[8,64,2048]{2,1,0:T(8,128)(2,1)} copy-done((bf16[8,64,2048]{2,1,0:T(8,128)(2,1)}, bf16[8,64,2048]{2,1,0:T(8,128)(2,1)S(1)}, u32[]{:S(2)}) %copy-start) | copy-done | bytes 2097176
  59.8 10.8 %encoder_partial.1 = bf16[512,2560]{1,0:T(8,128)(2,1)} custom-call(bf16[512,2048]{1,0:T(8,128)(2,1)} %bitcast.26, bf16[2560,512]{1,0:T(8,128)(2,1)} %bitcast.41, bf16[2560,512]{1,0:T(8,128)(2,1)} %bitcast.43, bf16[2560,512]{1,0:T(8,128)(2,1)} %collective-permute-done.okw_ref, bf16[2560,512]{1,0:T(8,128)(2,1)} %collective-permute-done.1.ovw_ref), custom_call_target="tpu_custom_call" | custom-call | flops 5368709120 | bytes 16777216 | tf_op jit(solution)/shard_map/encoder_partial/pallas_call | solution.py:97
  70.6 2.3 %slice.3 = bf16[512,1024]{1,0:T(8,128)(2,1)} slice(bf16[512,2048]{1,0:T(8,128)(2,1)} %bitcast.27), slice={[0:512], [1024:2048]} | slice | bytes 2097152 | tf_op jit(solution)/shard_map/slice | solution.py:256
  72.9 0.1 collective-permute-start.6
  72.9 10.5 %all-to-all-start.2 = ((bf16[64,8,2560]{2,1,0:T(8,128)(2,1)}), bf16[64,8,2560]{2,1,0:T(8,128)(2,1)S(1)}, u32[]{:S(2)}, u32[]{:S(2)}) async-start(bf16[64,8,2560]{2,1,0:T(8,128)(2,1)} %bitcast.29), calls=%async_computation.2 | async-start | bytes 5242880 | tf_op jit(solution)/shard_map/all_to_all | solution.py:254
  83.4 0.0 collective-permute-done.5.oe_ref
  83.4 0.0 collective-permute-done.6.okv_ref
  83.4 28.8 %updates.1 = (f32[2560,512]{1,0:T(8,128)}, f32[2560,512]{1,0:T(8,128)}) custom-call(bf16[512,2560]{1,0:T(8,128)(2,1)} %bitcast.18.e_ref, bf16[512,2560]{1,0:T(8,128)(2,1)} %collective-permute-done.5.oe_ref, bf16[512,2048]{1,0:T(8,128)(2,1)} %bitcast.28, bf16[512,1024]{1,0:T(8,128)(2,1)} %collective-permute-done.6.okv_ref), custom_call_target="tpu_custom_call" | custom-call | flops 20000000000 | bytes 20971520 | tf_op jit(solution)/shard_map/updates/pallas_call | solution.py:191
  112.2 6.0 %all-to-all-done.2 = bf16[64,8,2560]{2,1,0:T(8,128)(2,1)S(1)} async-done(((bf16[64,8,2560]{2,1,0:T(8,128)(2,1)}), bf16[64,8,2560]{2,1,0:T(8,128)(2,1)S(1)}, u32[]{:S(2)}, u32[]{:S(2)}) %all-to-all-start.2) | async-done | bytes 2621472 | tf_op jit(solution)/shard_map/all_to_all | solution.py:254
  118.2 1.0 convert_reduce_fusion
  (1 shorter events, 0.0 us)
Async XLA Ops:
  2.3 22.3 %all-to-all-start.1 = ((bf16[16,8,2560]{2,1,0:T(8,128)(2,1)}), bf16[16,8,2560]{2,1,0:T(8,128)(2,1)S(1)}, u32[]{:S(2)}, u32[]{:S(2)}) async-start(bf16[16,8,2560]{2,1,0:T(8,128)(2,1)} %broadcast_in_dim.33), calls=%async_computation.1 | async-start | bytes 1310720 | tf_op jit(solution)/shard_map/all_to_all | solution.py:238
  24.6 19.2 %collective-permute-start.2 = (bf16[8,16,2560]{2,1,0:T(8,128)(2,1)S(1)}, bf16[8,16,2560]{2,1,0:T(8,128)(2,1)S(1)}, u32[]{:S(2)}, u32[]{:S(2)}) collective-permute-start(bf16[8,16,2560]{2,1,0:T(8,128)(2,1)S(1)} %bitcast.30), channel_id=1, source_target_pairs={{0,4},{2,6},{4,0},{6,2},{1,5},{3,7},{5,1},{7,3},{8,12},{10,14},{12... | collective-permute-start | bytes 1966088 | tf_op jit(solution)/shard_map/ppermute | solution.py:221
  27.8 30.8 %all-to-all-start = ((bf16[8,64,2048]{2,1,0:T(8,128)(2,1)}), bf16[8,64,2048]{2,1,0:T(8,128)(2,1)S(1)}, u32[]{:S(2)}, u32[]{:S(2)}) async-start(bf16[8,64,2048]{2,1,0:T(8,128)(2,1)} %attention.1), calls=%async_computation | async-start | bytes 4194304 | tf_op jit(solution)/shard_map/all_to_all | solution.py:244
  33.3 23.9 %collective-permute-start.4 = (bf16[8,16,2560]{2,1,0:T(8,128)(2,1)S(1)}, bf16[8,16,2560]{2,1,0:T(8,128)(2,1)S(1)}, u32[]{:S(2)}, u32[]{:S(2)}) collective-permute-start(bf16[8,16,2560]{2,1,0:T(8,128)(2,1)S(1)} %bitcast.31), channel_id=1, source_target_pairs={{0,6},{2,0},{4,2},{6,4},{1,7},{3,1},{5,3},{7,5},{8,14},{10,8},{12,... | collective-permute-start | bytes 1966088 | tf_op jit(solution)/shard_map/ppermute | solution.py:221
  34.4 21.9 %collective-permute-start.3 = (bf16[8,16,2560]{2,1,0:T(8,128)(2,1)S(1)}, bf16[8,16,2560]{2,1,0:T(8,128)(2,1)S(1)}, u32[]{:S(2)}, u32[]{:S(2)}) collective-permute-start(bf16[8,16,2560]{2,1,0:T(8,128)(2,1)S(1)} %bitcast.32), channel_id=1, source_target_pairs={{0,2},{2,4},{4,6},{6,0},{1,3},{3,5},{5,7},{7,1},{8,10},{10,12},{12... | collective-permute-start | bytes 1966088 | tf_op jit(solution)/shard_map/ppermute | solution.py:221
  35.4 23.2 %collective-permute-start = (bf16[2560,512]{1,0:T(8,128)(2,1)}, bf16[2560,512]{1,0:T(8,128)(2,1)}, u32[]{:S(2)}, u32[]{:S(2)}) collective-permute-start(bf16[2560,512]{1,0:T(8,128)(2,1)} %bitcast.40), channel_id=1, source_target_pairs={{0,8},{8,0},{1,9},{9,1},{2,10},{10,2},{3,11},{11,3},{4,12},{12,4},... | collective-permute-start | bytes 7864328 | tf_op jit(solution)/shard_map/ppermute | solution.py:249
  35.4 23.2 %collective-permute-start.1 = (bf16[2560,512]{1,0:T(8,128)(2,1)}, bf16[2560,512]{1,0:T(8,128)(2,1)}, u32[]{:S(2)}, u32[]{:S(2)}) collective-permute-start(bf16[2560,512]{1,0:T(8,128)(2,1)} %bitcast.42), channel_id=1, source_target_pairs={{0,8},{8,0},{1,9},{9,1},{2,10},{10,2},{3,11},{11,3},{4,12},{12,4},... | collective-permute-start | bytes 7864328 | tf_op jit(solution)/shard_map/ppermute | solution.py:250
  58.1 25.3 %collective-permute-start.5 = (bf16[512,2560]{1,0:T(8,128)(2,1)}, bf16[512,2560]{1,0:T(8,128)(2,1)}, u32[]{:S(2)}, u32[]{:S(2)}) collective-permute-start(bf16[512,2560]{1,0:T(8,128)(2,1)} %bitcast.18.e_ref), channel_id=1, source_target_pairs={{0,8},{8,0},{1,9},{9,1},{2,10},{10,2},{3,11},{11,3},{4,12},{12,4},... | collective-permute-start | bytes 7864328 | tf_op jit(solution)/shard_map/ppermute | solution.py:251
  58.5 1.3 %copy-start = (bf16[8,64,2048]{2,1,0:T(8,128)(2,1)}, bf16[8,64,2048]{2,1,0:T(8,128)(2,1)S(1)}, u32[]{:S(2)}) copy-start(bf16[8,64,2048]{2,1,0:T(8,128)(2,1)S(1)} %all-to-all-done) | copy-start | bytes 6291460
  72.9 10.5 %collective-permute-start.6 = (bf16[512,1024]{1,0:T(8,128)(2,1)}, bf16[512,1024]{1,0:T(8,128)(2,1)}, u32[]{:S(2)}, u32[]{:S(2)}) collective-permute-start(bf16[512,1024]{1,0:T(8,128)(2,1)} %slice.3), channel_id=1, source_target_pairs={{0,8},{8,0},{1,9},{9,1},{2,10},{10,2},{3,11},{11,3},{4,12},{12,4},... | collective-permute-start | bytes 3145736 | tf_op jit(solution)/shard_map/ppermute | solution.py:256
  72.9 45.3 %all-to-all-start.2 = ((bf16[64,8,2560]{2,1,0:T(8,128)(2,1)}), bf16[64,8,2560]{2,1,0:T(8,128)(2,1)S(1)}, u32[]{:S(2)}, u32[]{:S(2)}) async-start(bf16[64,8,2560]{2,1,0:T(8,128)(2,1)} %bitcast.29), calls=%async_computation.2 | async-start | bytes 5242880 | tf_op jit(solution)/shard_map/all_to_all | solution.py:254

commit v2 on v1

v2 whole, which is shorter than its diff:
```python
import functools
import math

import jax
import jax.numpy as jnp
from jax import lax
from jax.experimental import pallas as pl
from jax.experimental.pallas import tpu as pltpu
from jax.sharding import Mesh, PartitionSpec as P

D = 2560
HEAD = 128
SWEEPS = 5

LINEAR_COEFF = 3.4445
SQUARE_COEFF = -4.775
CUBIC_COEFF = 2.0315

BF16 = jnp.bfloat16
F32 = jnp.float32
HIGHEST = lax.Precision.HIGHEST

MIB = 1024 * 1024


def dot(a, b, dims, precision=None):
    return lax.dot_general(a, b, (dims, ((), ())), precision=precision, preferred_element_type=F32)


def attention_kernel(place, lens, q_ref, k_ref, v_ref, g_ref, out_ref):
    src = k_ref.shape[0]
    tgt = q_ref.shape[0]
    group = out_ref.shape[2] // 4
    core = lax.rem(place[0], 2)
    row = lax.broadcasted_iota(jnp.int32, (src, tgt), 0)
    valid = (row < lens[place[0]]).astype(F32)
    scale = 1.0 / math.sqrt(HEAD)
    cols = [slice(h * HEAD, (h + 1) * HEAD) for h in range(q_ref.shape[1] // HEAD)]
    cat = jnp.concatenate
    both = [
        dot(cat([k_ref[:, c], v_ref[:, c]], 0), cat([q_ref[:, c], g_ref[:, c]], 0), ((1,), (1,))) for c in cols
    ]
    grad_probs = [b[src:, tgt:] for b in both]
    raw = [jnp.exp2(b[:src, :tgt] * (scale * math.log2(math.e))) * valid for b in both]
    probs = [r * (1.0 / jnp.sum(r, axis=0, keepdims=True)) for r in raw]
    delta = [jnp.sum(p * g, axis=0, keepdims=True) for p, g in zip(probs, grad_probs)]
    low = [
        cat([(p * ((g - d) * scale)).astype(BF16), p.astype(BF16)], 0)
        for p, g, d in zip(probs, grad_probs, delta)
    ]
    for h, c in enumerate(cols):
        grads = dot(low[h], cat([q_ref[:, c], g_ref[:, c]], 1), ((1,), (0,)))
        chip, of_core, at = h * HEAD // (2 * group), h * HEAD // group % 2, h * HEAD % group
        first = lax.bitwise_xor(core, of_core) * 2 * group + at
        out_ref[chip, :, pl.ds(pl.multiple_of(first, HEAD), HEAD)] = grads[:src, :HEAD].astype(BF16)
        out_ref[chip, :, pl.ds(pl.multiple_of(first + group, HEAD), HEAD)] = grads[src:, HEAD:].astype(BF16)


def attention(place, lens, q, k, v, g, chips, group):
    tgt, src = q.shape[0], k.shape[0]
    some = 2
    wide = 2 * group * some

    def col(p, place, lens):
        return (0, p)

    return pl.pallas_call(
        attention_kernel,
        grid_spec=pltpu.PrefetchScalarGridSpec(
            num_scalar_prefetch=2,
            grid=(chips // some,),
            in_specs=[
                pl.BlockSpec((tgt, wide), col),
                pl.BlockSpec((src, wide), col),
                pl.BlockSpec((src, wide), col),
                pl.BlockSpec((tgt, wide), col),
            ],
            out_specs=pl.BlockSpec((some, src, 4 * group), lambda p, place, lens: (p, 0, 0)),
        ),
        out_shape=jax.ShapeDtypeStruct((chips, src, 4 * group), BF16),
        compiler_params=pltpu.CompilerParams(vmem_limit_bytes=56 * MIB),
        cost_estimate=pl.CostEstimate(flops=700_000_000, bytes_accessed=8 * MIB, transcendentals=600_000),
        name="attention",
    )(place, lens, q, k, v, g)


def partial_kernel(kv_ref, kw_ref, vw_ref, okw_ref, ovw_ref, out_ref):
    w = kw_ref.shape[1]
    total = None
    for i, ref in enumerate((kw_ref, vw_ref, okw_ref, ovw_ref)):
        term = dot(kv_ref[:, i * w : (i + 1) * w], ref[...], ((1,), (1,)))
        total = term if total is None else total + term
    out_ref[...] = total.astype(BF16)


def encoder_partial(kv, kw, vw, okw, ovw):
    rows, feats = kv.shape
    width, w = kw.shape
    tile = 512
    spec = pl.BlockSpec((tile, w), lambda j: (j, 0))
    return pl.pallas_call(
        partial_kernel,
        grid=(width // tile,),
        in_specs=[pl.BlockSpec((rows, feats), lambda j: (0, 0)), spec, spec, spec, spec],
        out_specs=pl.BlockSpec((rows, tile), lambda j: (0, j)),
        out_shape=jax.ShapeDtypeStruct((rows, width), BF16),
        compiler_params=pltpu.CompilerParams(vmem_limit_bytes=56 * MIB),
        cost_estimate=pl.CostEstimate(
            flops=2 * rows * feats * width, bytes_accessed=16 * MIB, transcendentals=0
        ),
        name="encoder_partial",
    )(kv, kw, vw, okw, ovw)


def two_parts(x):
    high = x.astype(BF16)
    low = (x - high.astype(F32)).astype(BF16)
    return high, low


def update_kernel(y_shifts, spot, *refs):
    count = 2 * len(y_shifts)
    pieces, rest = refs[:count], refs[count:]
    kv_ref, okv_ref, key_ref, value_ref, lines, parts, gram, mix, result, sems = rest
    width = pieces[0].shape[1]
    inner = key_ref.shape[1]
    heads = inner // HEAD
    chunk = inner
    chunks = width // chunk

    row = lax.broadcasted_iota(jnp.int32, (HEAD, HEAD), 0)
    eye = (row == lax.broadcasted_iota(jnp.int32, (HEAD, HEAD), 1)).astype(F32)

    def prod(a, b):
        return dot(a, b, ((1,), (0,)), HIGHEST)

    def near_prod(a, b):
        left = jnp.concatenate(two_parts(a), axis=1)
        line = jnp.concatenate(two_parts(b), axis=1)
        full = dot(left, jnp.concatenate([line, line], axis=0), ((1,), (0,)))
        return full[:, :HEAD] + full[:, HEAD:]

    at = 0
    for ref in (kv_ref, okv_ref):
        for y in y_shifts:
            some = ref[:, lax.rem(spot[0] + (4 - y), 4)]
            some = some.reshape(-1, some.shape[2])
            lines[:, at : at + some.shape[0]] = some.T
            at += some.shape[0]

    def lanes(i):
        return slice(i * chunk, (i + 1) * chunk)

    def sums(first, i):
        rows = jnp.concatenate([ref[:, lanes(i)] for ref in pieces], axis=0)
        total = dot(lines[first * HEAD : (first + heads) * HEAD], rows, ((1,), (0,)))
        for h in range(heads):
            both = jnp.concatenate(two_parts(total[h * HEAD : (h + 1) * HEAD]), axis=0)
            parts[first + h, :, lanes(i)] = both
            full = dot(both, both, ((1,), (1,)))
            term = (full[:HEAD, :HEAD] + full[HEAD:, HEAD:]) + (full[:HEAD, HEAD:] + full[HEAD:, :HEAD])
            gram[first + h] = gram[first + h] + term

    def start(first):
        for h in range(first, first + heads):
            whole = gram[h]
            trace = jnp.sum(jnp.sum(whole * eye, axis=1, keepdims=True), axis=0, keepdims=True)
            inverse = 1.0 / (jnp.sqrt(trace) + 1e-07)
            gram[h] = whole * inverse * inverse
            mix[h] = eye * (inverse * math.sqrt(width))

    def sweep(first, last):
        grams = [gram[first + h] for h in range(heads)]
        squares = [near_prod(a, a) for a in grams]
        steps = [LINEAR_COEFF * eye + (SQUARE_COEFF * a + CUBIC_COEFF * s) for a, s in zip(grams, squares)]
        mixes = [near_prod(mix[first + h], m) for h, m in enumerate(steps)]
        for h in range(heads):
            mix[first + h] = mixes[h]
        if not last:
            halves = [prod(a, m) for a, m in zip(grams, steps)]
            nexts = [prod(m, a) for a, m in zip(halves, steps)]
            for h in range(heads):
                gram[first + h] = nexts[h]

    def leave(first, i, ref):
        rows = lanes(i)
        place = 0 if first == 0 else 1
        return pltpu.make_async_copy(result.at[place, rows], ref.at[rows], sems.at[place, i])

    def finish(first, i, ref):
        place = 0 if first == 0 else 1
        for h in range(heads):
            line = jnp.concatenate(two_parts(mix[first + h]), axis=1)
            right = jnp.concatenate([line, line], axis=0)
            out = dot(parts[first + h, :, lanes(i)], right, ((0,), (0,)))
            result[place, lanes(i), h * HEAD : (h + 1) * HEAD] = out[:, :HEAD] + out[:, HEAD:]
        leave(first, i, ref).start()

    gram[...] = jnp.zeros_like(gram)

    for i in range(chunks):
        sums(0, i)
    start(0)
    for i in range(SWEEPS):
        sums(heads, i)
        sweep(0, i == SWEEPS - 1)
    start(heads)
    for i in range(SWEEPS):
        finish(0, i, key_ref)
        sweep(heads, i == SWEEPS - 1)
    for i in range(chunks):
        finish(heads, i, value_ref)
    for i in range(chunks):
        leave(0, i, key_ref).wait()
        leave(heads, i, value_ref).wait()


def updates(spot, y_shifts, pieces, kv, okv, inner):
    rows, width = pieces[0].shape
    blocks, size, block = kv.shape[:3]
    heads = 2 * inner // HEAD
    chunks = width // inner
    assert chunks == SWEEPS
    whole = pl.BlockSpec((rows, width), lambda i, spot: (0, 0))

    def half(at):
        return pl.BlockSpec((blocks, size, block, 2 * inner), lambda i, spot: (0, 0, 0, at))

    return pl.pallas_call(
        functools.partial(update_kernel, y_shifts),
        grid_spec=pltpu.PrefetchScalarGridSpec(
            num_scalar_prefetch=1,
            grid=(1,),
            in_specs=[whole] * len(pieces) + [half(0), half(1)],
            out_specs=[pl.BlockSpec(memory_space=pl.ANY)] * 2,
            scratch_shapes=[
                pltpu.VMEM((2 * inner, 2 * blocks * size * block), BF16),
                pltpu.VMEM((heads, 2 * HEAD, width), BF16),
                pltpu.VMEM((heads, HEAD, HEAD), F32),
                pltpu.VMEM((heads, HEAD, HEAD), F32),
                pltpu.VMEM((2, width, inner), F32),
                pltpu.SemaphoreType.DMA((2, chunks)),
            ],
        ),
        out_shape=[jax.ShapeDtypeStruct((width, inner), F32)] * 2,
        compiler_params=pltpu.CompilerParams(vmem_limit_bytes=56 * MIB),
        cost_estimate=pl.CostEstimate(
            flops=20_000_000_000, bytes_accessed=20 * MIB, transcendentals=0
        ),
        name="updates",
    )(spot, *pieces, kv, okv)


def ring(shift):
    return [(j, (j + shift) % 4) for j in range(4)]


def body(
    encoded, source_len, queries, saved_keys, saved_values, out_grad, key_weight, value_weight
):
    across = [(0, 1), (1, 0)]
    key_weight, value_weight = key_weight[0], value_weight[0]
    width, inner = key_weight.shape
    block = encoded.shape[1]

    spread = jnp.broadcast_to(encoded, (16, block, width))
    near = lax.all_to_all(spread, ("xl", "z", "xh"), split_axis=0, concat_axis=0, tiled=True)
    near = near.reshape(16 * block, width)

    place = lax.axis_index(("xl", "z", "c")).astype(jnp.int32).reshape(1)
    local = attention(
        place, source_len, queries[0, 0], saved_keys[0, 0], saved_values[0, 0], out_grad[0, 0], 8, inner
    )
    moved = lax.all_to_all(local, ("xl", "z"), split_axis=0, concat_axis=0, tiled=True)

    near, key_send, value_send, _ = lax.optimization_barrier((near, key_weight, value_weight, local))
    shifts = (0, 2, 1, 3)
    own_rows = [near] + [lax.ppermute(near, "y", ring(s)) for s in shifts[1:]]
    other_kw = lax.ppermute(key_send, "c", across)
    other_vw = lax.ppermute(value_send, "c", across)

    moved, own_rows[2], own_rows[3] = lax.optimization_barrier((moved, own_rows[2], own_rows[3]))
    rows = moved.reshape(8 * local.shape[1], 4 * inner)
    other_rows = [lax.ppermute(r, "c", across) for r in own_rows]
    other_moved = lax.ppermute(moved, "c", across)
    partial = encoder_partial(rows, key_weight, value_weight, other_kw, other_vw)
    terms = lax.all_to_all(
        partial, ("xl", "z", "y", "xh"), split_axis=0, concat_axis=0, tiled=True
    )

    spot = lax.axis_index("y").astype(jnp.int32).reshape(1)
    by_y = (8, 4, 2 * block, 4 * inner)
    key_update, value_update = updates(
        spot, shifts, own_rows + other_rows, moved.reshape(by_y), other_moved.reshape(by_y), inner
    )
    encoder_grad = jnp.sum(terms.reshape(64, block, width).astype(F32), axis=0)
    return encoder_grad[None], key_update[None], value_update[None]


def solution(mesh):
    fine = Mesh(mesh.devices.reshape(2, 4, 2, 4, 2), ("xl", "z", "c", "y", "xh"))
    dp, section = ("xl", "z", "c"), ("y", "xh")
    in_specs = (
        P(dp, section, None),
        P(),
        P(section, dp, None, None),
        P(section, dp, None, None),
        P(section, dp, None, None),
        P(section, dp, None, None),
        P(section, None, dp),
        P(section, None, dp),
    )
    out_specs = (P(dp, section, None), P(section, None, dp), P(section, None, dp))
    return jax.shard_map(body, mesh=fine, in_specs=in_specs, out_specs=out_specs, check_vma=False)
```

time: 120 us -> 108 us (0.900)
  Pallas kernels: 53.8 us -> 40.7 us
  waiting for transfers between devices: 23.2 us -> 35.8 us
  local copies, waits for them, and re-layouts: 10.6 us -> 2.5 us
  starting transfers between devices: 29.8 us -> 27 us
    pallas_call x1, Pallas kernels: 14.3 us -> 6.92 us  [attention(): pl.pallas_call(attention_kernel, grid_spec=pltpu.PrefetchScalarGridSpec(n...]
    pallas_call x1, Pallas kernels: 28.8 us -> 23 us  [updates(): pl.pallas_call(functools.partial(update_kernel, y_shifts), grid_spec=pltp...]
    all_to_all x1, waiting for transfers between devices: 0.01 us -> 5.37 us  [body(): lax.all_to_all(spread, ('xl', 'z', 'xh'), split_axis=0, concat_axis=0, ti...]
    ppermute x5 -> x8, waiting for transfers between devices: 16.8 us -> 21.2 us  [the longest x3 16.9 us: body(): own_rows = [near] + [lax.ppermute(near, 'y', ring(s)) for s in shifts[1:]]]
    all_to_all x1, starting transfers between devices: 10.5 us -> 6.74 us  [body(): lax.all_to_all(partial, ('xl', 'z', 'y', 'xh'), split_axis=0, concat_axis...]
    dynamic_update_slice x4 -> x0, local copies, waits for them, and re-layouts: 3.6 us -> none  [gather_ring(): lax.dynamic_update_index_in_dim(out, piece, lax.rem(own - shift + size, s...]
    all_to_all x1, waiting for transfers between devices: 0.43 us -> 2.82 us  [body(): lax.all_to_all(local, ('xl', 'z'), split_axis=0, concat_axis=0, tiled=True)]
    slice x1 -> x0, local copies, waits for them, and re-layouts: 2.26 us -> none  [body(): other_kv = lax.ppermute(held[:, 2 * inner:], 'c', across)]
  transfers between devices with their start and end apart: 10 -> 13, of which waited for: 4 -> 9; matrix products, arithmetic and copies ran while one was open for 6% -> 0% of each run, Pallas kernels for 45% -> 38%
where the time goes in v2:
time: 108 us
  Pallas kernels  40.7 us (38%)
  waiting for transfers between devices  35.8 us (33%)
  starting transfers between devices  27 us (25%)
  local copies, waits for them, and re-layouts  2.5 us (2%)
    pallas_call x1, Pallas kernels, updates(): pl.pallas_call(functools.partial(update_kernel, y_shifts), grid_spec=pltp...  23 us
    ppermute x3, waiting for transfers between devices, body(): own_rows = [near] + [lax.ppermute(near, 'y', ring(s)) for s in shifts[1:]]  16.9 us
    pallas_call x1, Pallas kernels, encoder_partial(): pl.pallas_call(partial_kernel, grid=(width // tile,), in_specs=[pl.BlockS...  10.7 us
    all_to_all x1, starting transfers between devices, body(): lax.all_to_all(spread, ('xl', 'z', 'xh'), split_axis=0, concat_axis=0, ti...  7.96 us
    pallas_call x1, Pallas kernels, attention(): pl.pallas_call(attention_kernel, grid_spec=pltpu.PrefetchScalarGridSpec(n...  6.92 us
    all_to_all x1, starting transfers between devices, body(): lax.all_to_all(partial, ('xl', 'z', 'y', 'xh'), split_axis=0, concat_axis...  6.74 us
    all_to_all x1, waiting for transfers between devices, body(): lax.all_to_all(partial, ('xl', 'z', 'y', 'xh'), split_axis=0, concat_axis...  6.46 us
    ppermute x3, starting transfers between devices, body(): own_rows = [near] + [lax.ppermute(near, 'y', ring(s)) for s in shifts[1:]]  6.21 us
  transfers between devices with their start and end apart: 13, of which 9 were waited for; matrix products, arithmetic and copies ran while one was open for 0% of the time, Pallas kernels for 38%

profile of v2, /device:TPU:0, one launch (start us, length us, event | category | flops | bytes accessed | tf_op | source)
XLA Modules:
  0.0 107.7 jit_solution(7108573345629941720)
XLA Ops:
  0.6 1.7 %broadcast_in_dim.17 = bf16[16,8,2560]{2,1,0:T(8,128)(2,1)} broadcast(bf16[8,2560]{1,0:T(8,128)(2,1)} %bitcast.28), dimensions={1,2} | broadcast | bytes 696320 | tf_op jit(solution)/shard_map/broadcast_in_dim | solution.py:266
  2.3 8.0 %all-to-all-start.1 = ((bf16[16,8,2560]{2,1,0:T(8,128)(2,1)}), bf16[16,8,2560]{2,1,0:T(8,128)(2,1)S(1)}, u32[]{:S(2)}, u32[]{:S(2)}) async-start(bf16[16,8,2560]{2,1,0:T(8,128)(2,1)} %broadcast_in_dim.17), calls=%async_computation.1 | async-start | bytes 1310720 | tf_op jit(solution)/shard_map/all_to_all | solution.py:267
  10.3 6.9 %attention.1 = bf16[8,64,2048]{2,1,0:T(8,128)(2,1)} custom-call(s32[1]{0:T(128)} %bitcast.place, s32[16]{0:T(128)} %lens.1, bf16[128,8192]{1,0:T(8,128)(2,1)} %bitcast.18, bf16[64,8192]{1,0:T(8,128)(2,1)} %bitcast.20, bf16[64,8192]{1,0:T(8,128)(2,1)} %bitcast.21, bf16[128,8192]{1,0:T(8,128)(2,1)} %bitcast.19), custom_call_target="tpu_custom_call" | custom-call | flops 700000000 | bytes 8388608 | tf_op jit(solution)/shard_map/attention/pallas_call | solution.py:67
  17.2 5.4 %all-to-all-done.1 = bf16[16,8,2560]{2,1,0:T(8,128)(2,1)S(1)} async-done(((bf16[16,8,2560]{2,1,0:T(8,128)(2,1)}), bf16[16,8,2560]{2,1,0:T(8,128)(2,1)S(1)}, u32[]{:S(2)}, u32[]{:S(2)}) %all-to-all-start.1) | async-done | bytes 655392 | tf_op jit(solution)/shard_map/all_to_all | solution.py:267
  22.6 4.4 %all-to-all-start = ((bf16[8,64,2048]{2,1,0:T(8,128)(2,1)}), bf16[8,64,2048]{2,1,0:T(8,128)(2,1)}, u32[]{:S(2)}, u32[]{:S(2)}) async-start(bf16[8,64,2048]{2,1,0:T(8,128)(2,1)} %attention.1), calls=%async_computation | async-start | bytes 4194304 | tf_op jit(solution)/shard_map/all_to_all | solution.py:274
  26.9 0.1 collective-permute-start.2
  27.0 0.5 collective-permute-start.3
  27.5 3.0 %collective-permute-start.1 = (bf16[128,2560]{1,0:T(8,128)(2,1)S(1)}, bf16[128,2560]{1,0:T(8,128)(2,1)S(1)}, u32[]{:S(2)}, u32[]{:S(2)}) collective-permute-start(bf16[128,2560]{1,0:T(8,128)(2,1)S(1)} %bitcast.22), channel_id=1, source_target_pairs={{0,6},{2,0},{4,2},{6,4},{1,7},{3,1},{5,3},{7,5},{8,14},{10,8},{12,... | collective-permute-start | bytes 1966088 | tf_op jit(solution)/shard_map/ppermute | solution.py:278
  30.6 0.0 collective-permute-start
  30.6 14.2 %collective-permute-done.1.refs_3_ = bf16[128,2560]{1,0:T(8,128)(2,1)S(1)} collective-permute-done((bf16[128,2560]{1,0:T(8,128)(2,1)S(1)}, bf16[128,2560]{1,0:T(8,128)(2,1)S(1)}, u32[]{:S(2)}, u32[]{:S(2)}) %collective-permute-start.1) | collective-permute-done | bytes 655392 | tf_op jit(solution)/shard_map/ppermute | solution.py:278
  44.8 0.8 copy-done.2
  45.6 2.7 %collective-permute-done.refs_2_ = bf16[128,2560]{1,0:T(8,128)(2,1)} collective-permute-done((bf16[128,2560]{1,0:T(8,128)(2,1)S(1)}, bf16[128,2560]{1,0:T(8,128)(2,1)}, u32[]{:S(2)}, u32[]{:S(2)}) %collective-permute-start) | collective-permute-done | bytes 655392 | tf_op jit(solution)/shard_map/ppermute | solution.py:278
  48.3 2.8 %all-to-all-done = bf16[8,64,2048]{2,1,0:T(8,128)(2,1)} async-done(((bf16[8,64,2048]{2,1,0:T(8,128)(2,1)}), bf16[8,64,2048]{2,1,0:T(8,128)(2,1)}, u32[]{:S(2)}, u32[]{:S(2)}) %all-to-all-start) | async-done | bytes 2097184 | tf_op jit(solution)/shard_map/all_to_all | solution.py:274
  51.1 0.0 collective-permute-start.9
  51.1 3.2 %collective-permute-start.4 = (bf16[128,2560]{1,0:T(8,128)(2,1)S(1)}, bf16[128,2560]{1,0:T(8,128)(2,1)}, u32[]{:S(2)}, u32[]{:S(2)}) collective-permute-start(bf16[128,2560]{1,0:T(8,128)(2,1)S(1)} %bitcast.24), channel_id=1, source_target_pairs={{0,4},{2,6},{4,0},{6,2},{1,5},{3,7},{5,1},{7,3},{8,12},{10,14},{12... | collective-permute-start | bytes 1966088 | tf_op jit(solution)/shard_map/ppermute | solution.py:278
  54.3 0.0 collective-permute-done.2.okw_ref
  54.3 0.0 collective-permute-done.3.ovw_ref
  54.3 10.7 %encoder_partial.1 = bf16[512,2560]{1,0:T(8,128)(2,1)} custom-call(bf16[512,2048]{1,0:T(8,128)(2,1)} %bitcast.9.kv_ref, bf16[2560,512]{1,0:T(8,128)(2,1)} %bitcast.29, bf16[2560,512]{1,0:T(8,128)(2,1)} %bitcast.32, bf16[2560,512]{1,0:T(8,128)(2,1)} %collective-permute-done.2.okw_ref, bf16[2560,512]{1,0:T(8,128)(2,1)} %collective-permute-done.3.ovw_ref), custom_call_target="tpu_custom_call" | custom-call | flops 5368709120 | bytes 16777216 | tf_op jit(solution)/shard_map/encoder_partial/pallas_call | solution.py:101
  65.0 6.7 %all-to-all-start.2 = ((bf16[64,8,2560]{2,1,0:T(8,128)(2,1)}), bf16[64,8,2560]{2,1,0:T(8,128)(2,1)S(1)}, u32[]{:S(2)}, u32[]{:S(2)}) async-start(bf16[64,8,2560]{2,1,0:T(8,128)(2,1)} %bitcast.17), calls=%async_computation.2 | async-start | bytes 5242880 | tf_op jit(solution)/shard_map/all_to_all | solution.py:287
  71.8 0.1 collective-permute-start.5
  71.9 0.0 collective-permute-done.4.refs_1_
  71.9 0.5 collective-permute-start.6
  72.4 0.1 collective-permute-start.7
  72.5 0.4 collective-permute-start.8
  72.9 1.2 %collective-permute-done.5.refs_4_ = bf16[128,2560]{1,0:T(8,128)(2,1)} collective-permute-done((bf16[128,2560]{1,0:T(8,128)(2,1)S(1)}, bf16[128,2560]{1,0:T(8,128)(2,1)}, u32[]{:S(2)}, u32[]{:S(2)}) %collective-permute-start.5) | collective-permute-done | bytes 655392 | tf_op jit(solution)/shard_map/ppermute | solution.py:284
  74.1 1.1 %collective-permute-done.6.refs_5_ = bf16[128,2560]{1,0:T(8,128)(2,1)} collective-permute-done((bf16[128,2560]{1,0:T(8,128)(2,1)}, bf16[128,2560]{1,0:T(8,128)(2,1)}, u32[]{:S(2)}, u32[]{:S(2)}) %collective-permute-start.6) | collective-permute-done | bytes 655392 | tf_op jit(solution)/shard_map/ppermute | solution.py:284
  75.3 0.9 collective-permute-done.7.refs_6_
  76.2 0.9 collective-permute-done.8.refs_7_
  77.1 0.0 collective-permute-done.9
  77.1 23.0 %updates.1 = (f32[2560,512]{1,0:T(8,128)}, f32[2560,512]{1,0:T(8,128)}) custom-call(s32[1]{0:T(128)} %bitcast.12.spot, bf16[128,2560]{1,0:T(8,128)(2,1)} %bitcast.26, bf16[128,2560]{1,0:T(8,128)(2,1)} %collective-permute-done.4.refs_1_, bf16[128,2560]{1,0:T(8,128)(2,1)} %collective-permute-done.refs_2_, bf16[128,2560]{1,0:T(8,128)(2,1)} %copy-done.2, ...), custom_call_target="tpu_custom_call" | custom-call | flops 20000000000 | bytes 20971520 | tf_op jit(solution)/shard_map/updates/pallas_call | solution.py:229
  100.2 6.5 %all-to-all-done.2 = bf16[64,8,2560]{2,1,0:T(8,128)(2,1)S(1)} async-done(((bf16[64,8,2560]{2,1,0:T(8,128)(2,1)}), bf16[64,8,2560]{2,1,0:T(8,128)(2,1)S(1)}, u32[]{:S(2)}, u32[]{:S(2)}) %all-to-all-start.2) | async-done | bytes 2621472 | tf_op jit(solution)/shard_map/all_to_all | solution.py:287
  106.6 1.0 convert_reduce_fusion
  (5 shorter events, 0.0 us)
Async XLA Ops:
  2.3 20.3 %all-to-all-start.1 = ((bf16[16,8,2560]{2,1,0:T(8,128)(2,1)}), bf16[16,8,2560]{2,1,0:T(8,128)(2,1)S(1)}, u32[]{:S(2)}, u32[]{:S(2)}) async-start(bf16[16,8,2560]{2,1,0:T(8,128)(2,1)} %broadcast_in_dim.17), calls=%async_computation.1 | async-start | bytes 1310720 | tf_op jit(solution)/shard_map/all_to_all | solution.py:267
  17.2 9.8 %copy-start.1 = (bf16[1,2560,512]{2,1,0:T(8,128)(2,1)S(1)}, bf16[1,2560,512]{2,1,0:T(8,128)(2,1)}, u32[]{:S(2)}) copy-start(bf16[1,2560,512]{2,1,0:T(8,128)(2,1)} %param.14) | copy-start | bytes 7864324
  22.6 49.2 %copy-start = (bf16[16,8,2560]{2,1,0:T(8,128)(2,1)}, bf16[16,8,2560]{2,1,0:T(8,128)(2,1)S(1)}, u32[]{:S(2)}) copy-start(bf16[16,8,2560]{2,1,0:T(8,128)(2,1)S(1)} %all-to-all-done.1) | copy-start | bytes 1966084
  22.6 28.6 %all-to-all-start = ((bf16[8,64,2048]{2,1,0:T(8,128)(2,1)}), bf16[8,64,2048]{2,1,0:T(8,128)(2,1)}, u32[]{:S(2)}, u32[]{:S(2)}) async-start(bf16[8,64,2048]{2,1,0:T(8,128)(2,1)} %attention.1), calls=%async_computation | async-start | bytes 4194304 | tf_op jit(solution)/shard_map/all_to_all | solution.py:274
  26.9 27.4 %collective-permute-start.2 = (bf16[2560,512]{1,0:T(8,128)(2,1)S(1)}, bf16[2560,512]{1,0:T(8,128)(2,1)}, u32[]{:S(2)}, u32[]{:S(2)}) collective-permute-start(bf16[2560,512]{1,0:T(8,128)(2,1)S(1)} %bitcast.30), channel_id=1, source_target_pairs={{0,8},{8,0},{1,9},{9,1},{2,10},{10,2},{3,11},{11,3},{4,12},{12,4},... | collective-permute-start | bytes 7864328 | tf_op jit(solution)/shard_map/ppermute | solution.py:279
  27.0 27.3 %collective-permute-start.3 = (bf16[2560,512]{1,0:T(8,128)(2,1)}, bf16[2560,512]{1,0:T(8,128)(2,1)}, u32[]{:S(2)}, u32[]{:S(2)}) collective-permute-start(bf16[2560,512]{1,0:T(8,128)(2,1)} %bitcast.31), channel_id=1, source_target_pairs={{0,8},{8,0},{1,9},{9,1},{2,10},{10,2},{3,11},{11,3},{4,12},{12,4},... | collective-permute-start | bytes 7864328 | tf_op jit(solution)/shard_map/ppermute | solution.py:280
  27.5 17.3 %collective-permute-start.1 = (bf16[128,2560]{1,0:T(8,128)(2,1)S(1)}, bf16[128,2560]{1,0:T(8,128)(2,1)S(1)}, u32[]{:S(2)}, u32[]{:S(2)}) collective-permute-start(bf16[128,2560]{1,0:T(8,128)(2,1)S(1)} %bitcast.22), channel_id=1, source_target_pairs={{0,6},{2,0},{4,2},{6,4},{1,7},{3,1},{5,3},{7,5},{8,14},{10,8},{12,... | collective-permute-start | bytes 1966088 | tf_op jit(solution)/shard_map/ppermute | solution.py:278
  30.6 17.8 %collective-permute-start = (bf16[128,2560]{1,0:T(8,128)(2,1)S(1)}, bf16[128,2560]{1,0:T(8,128)(2,1)}, u32[]{:S(2)}, u32[]{:S(2)}) collective-permute-start(bf16[128,2560]{1,0:T(8,128)(2,1)S(1)} %bitcast.23), channel_id=1, source_target_pairs={{0,2},{2,4},{4,6},{6,0},{1,3},{3,5},{5,7},{7,1},{8,10},{10,12},{12... | collective-permute-start | bytes 1966088 | tf_op jit(solution)/shard_map/ppermute | solution.py:278
  44.8 0.8 copy-start.2
  51.1 26.0 %collective-permute-start.9 = (bf16[8,64,2048]{2,1,0:T(8,128)(2,1)}, bf16[8,64,2048]{2,1,0:T(8,128)(2,1)}, u32[]{:S(2)}, u32[]{:S(2)}) collective-permute-start(bf16[8,64,2048]{2,1,0:T(8,128)(2,1)} %all-to-all-done), channel_id=1, source_target_pairs={{0,8},{8,0},{1,9},{9,1},{2,10},{10,2},{3,11},{11,3},{4,12},{12,4},... | collective-permute-start | bytes 6291464 | tf_op jit(solution)/shard_map/ppermute | solution.py:285
  51.1 20.8 %collective-permute-start.4 = (bf16[128,2560]{1,0:T(8,128)(2,1)S(1)}, bf16[128,2560]{1,0:T(8,128)(2,1)}, u32[]{:S(2)}, u32[]{:S(2)}) collective-permute-start(bf16[128,2560]{1,0:T(8,128)(2,1)S(1)} %bitcast.24), channel_id=1, source_target_pairs={{0,4},{2,6},{4,0},{6,2},{1,5},{3,7},{5,1},{7,3},{8,12},{10,14},{12... | collective-permute-start | bytes 1966088 | tf_op jit(solution)/shard_map/ppermute | solution.py:278
  65.0 41.6 %all-to-all-start.2 = ((bf16[64,8,2560]{2,1,0:T(8,128)(2,1)}), bf16[64,8,2560]{2,1,0:T(8,128)(2,1)S(1)}, u32[]{:S(2)}, u32[]{:S(2)}) async-start(bf16[64,8,2560]{2,1,0:T(8,128)(2,1)} %bitcast.17), calls=%async_computation.2 | async-start | bytes 5242880 | tf_op jit(solution)/shard_map/all_to_all | solution.py:287
  71.8 2.3 %collective-permute-start.5 = (bf16[128,2560]{1,0:T(8,128)(2,1)S(1)}, bf16[128,2560]{1,0:T(8,128)(2,1)}, u32[]{:S(2)}, u32[]{:S(2)}) collective-permute-start(bf16[128,2560]{1,0:T(8,128)(2,1)S(1)} %bitcast.25), channel_id=1, source_target_pairs={{0,8},{8,0},{1,9},{9,1},{2,10},{10,2},{3,11},{11,3},{4,12},{12,4},... | collective-permute-start | bytes 1966088 | tf_op jit(solution)/shard_map/ppermute | solution.py:284
  71.9 3.4 %collective-permute-start.6 = (bf16[128,2560]{1,0:T(8,128)(2,1)}, bf16[128,2560]{1,0:T(8,128)(2,1)}, u32[]{:S(2)}, u32[]{:S(2)}) collective-permute-start(bf16[128,2560]{1,0:T(8,128)(2,1)} %collective-permute-done.4.refs_1_), channel_id=1, source_target_pairs={{0,8},{8,0},{1,9},{9,1},{2,10},{10,2},{3,11},{11,3},{4,12},{12,4},... | collective-permute-start | bytes 1966088 | tf_op jit(solution)/shard_map/ppermute | solution.py:284
  72.4 3.8 %collective-permute-start.7 = (bf16[128,2560]{1,0:T(8,128)(2,1)}, bf16[128,2560]{1,0:T(8,128)(2,1)}, u32[]{:S(2)}, u32[]{:S(2)}) collective-permute-start(bf16[128,2560]{1,0:T(8,128)(2,1)} %collective-permute-done.refs_2_), channel_id=1, source_target_pairs={{0,8},{8,0},{1,9},{9,1},{2,10},{10,2},{3,11},{11,3},{4,12},{12,4},... | collective-permute-start | bytes 1966088 | tf_op jit(solution)/shard_map/ppermute | solution.py:284
  72.5 4.6 %collective-permute-start.8 = (bf16[128,2560]{1,0:T(8,128)(2,1)}, bf16[128,2560]{1,0:T(8,128)(2,1)}, u32[]{:S(2)}, u32[]{:S(2)}) collective-permute-start(bf16[128,2560]{1,0:T(8,128)(2,1)} %copy-done.2), channel_id=1, source_target_pairs={{0,8},{8,0},{1,9},{9,1},{2,10},{10,2},{3,11},{11,3},{4,12},{12,4},... | collective-permute-start | bytes 1966088 | tf_op jit(solution)/shard_map/ppermute | solution.py:284

commit v3 on v2

--- a/solution.py
+++ b/solution.py
@@ -27,7 +27,8 @@
     return lax.dot_general(a, b, (dims, ((), ())), precision=precision, preferred_element_type=F32)
 
 
-def attention_kernel(place, lens, q_ref, k_ref, v_ref, g_ref, out_ref):
+def attention_kernel(place, lens, q_ref, k_ref, v_ref, g_ref, *refs):
+    out_ref = refs[-1]
     src = k_ref.shape[0]
     tgt = q_ref.shape[0]
     group = out_ref.shape[2] // 4
@@ -56,32 +57,35 @@
         out_ref[chip, :, pl.ds(pl.multiple_of(first + group, HEAD), HEAD)] = grads[src:, HEAD:].astype(BF16)
 
 
-def attention(place, lens, q, k, v, g, chips, group):
+def attention(place, lens, q, k, v, g, chips, group, first, count, earlier=None):
     tgt, src = q.shape[0], k.shape[0]
     some = 2
     wide = 2 * group * some
+    begin = first // some
 
     def col(p, place, lens):
-        return (0, p)
+        return (0, begin + p)
 
     return pl.pallas_call(
         attention_kernel,
         grid_spec=pltpu.PrefetchScalarGridSpec(
             num_scalar_prefetch=2,
-            grid=(chips // some,),
+            grid=(count // some,),
             in_specs=[
                 pl.BlockSpec((tgt, wide), col),
                 pl.BlockSpec((src, wide), col),
                 pl.BlockSpec((src, wide), col),
                 pl.BlockSpec((tgt, wide), col),
-            ],
-            out_specs=pl.BlockSpec((some, src, 4 * group), lambda p, place, lens: (p, 0, 0)),
+            ]
+            + ([] if earlier is None else [pl.BlockSpec(memory_space=pl.ANY)]),
+            out_specs=pl.BlockSpec((some, src, 4 * group), lambda p, place, lens: (begin + p, 0, 0)),
         ),
         out_shape=jax.ShapeDtypeStruct((chips, src, 4 * group), BF16),
+        input_output_aliases={} if earlier is None else {6: 0},
         compiler_params=pltpu.CompilerParams(vmem_limit_bytes=56 * MIB),
-        cost_estimate=pl.CostEstimate(flops=700_000_000, bytes_accessed=8 * MIB, transcendentals=600_000),
+        cost_estimate=pl.CostEstimate(flops=350_000_000, bytes_accessed=4 * MIB, transcendentals=300_000),
         name="attention",
-    )(place, lens, q, k, v, g)
+    )(place, lens, q, k, v, g, *([] if earlier is None else [earlier]))
 
 
 def partial_kernel(kv_ref, kw_ref, vw_ref, okw_ref, ovw_ref, out_ref):
@@ -118,7 +122,7 @@
     return high, low
 
 
-def update_kernel(y_shifts, spot, *refs):
+def update_kernel(z_shifts, y_shifts, spot, *refs):
     count = 2 * len(y_shifts)
     pieces, rest = refs[:count], refs[count:]
     kv_ref, okv_ref, key_ref, value_ref, lines, parts, gram, mix, result, sems = rest
@@ -143,8 +147,15 @@
     at = 0
     for ref in (kv_ref, okv_ref):
         for y in y_shifts:
-            some = ref[:, lax.rem(spot[0] + (4 - y), 4)]
-            some = some.reshape(-1, some.shape[2])
+            of_y = lax.rem(spot[2] + (4 - y), 4)
+            some = jnp.concatenate(
+                [
+                    ref[lax.bitwise_xor(spot[0], x) * 4 + lax.rem(spot[1] + (4 - z), 4), of_y]
+                    for z in z_shifts
+                    for x in range(2)
+                ],
+                axis=0,
+            )
             lines[:, at : at + some.shape[0]] = some.T
             at += some.shape[0]
 
@@ -215,7 +226,7 @@
         leave(heads, i, value_ref).wait()
 
 
-def updates(spot, y_shifts, pieces, kv, okv, inner):
+def updates(spot, z_shifts, y_shifts, pieces, kv, okv, inner):
     rows, width = pieces[0].shape
     blocks, size, block = kv.shape[:3]
     heads = 2 * inner // HEAD
@@ -227,7 +238,7 @@
         return pl.BlockSpec((blocks, size, block, 2 * inner), lambda i, spot: (0, 0, 0, at))
 
     return pl.pallas_call(
-        functools.partial(update_kernel, y_shifts),
+        functools.partial(update_kernel, z_shifts, y_shifts),
         grid_spec=pltpu.PrefetchScalarGridSpec(
             num_scalar_prefetch=1,
             grid=(1,),
@@ -263,17 +274,24 @@
     width, inner = key_weight.shape
     block = encoded.shape[1]
 
-    spread = jnp.broadcast_to(encoded, (16, block, width))
-    near = lax.all_to_all(spread, ("xl", "z", "xh"), split_axis=0, concat_axis=0, tiled=True)
-    near = near.reshape(16 * block, width)
-
     place = lax.axis_index(("xl", "z", "c")).astype(jnp.int32).reshape(1)
-    local = attention(
-        place, source_len, queries[0, 0], saved_keys[0, 0], saved_values[0, 0], out_grad[0, 0], 8, inner
-    )
+    given = (queries[0, 0], saved_keys[0, 0], saved_values[0, 0], out_grad[0, 0])
+    across_x = lax.ppermute(encoded[0], "xh", across)
+    local = attention(place, source_len, *given, 8, inner, 0, 2)
+    across_x, local = lax.optimization_barrier((across_x, local))
+    low = lax.axis_index("xh") == 0
+    pair = jnp.concatenate([jnp.where(low, encoded[0], across_x), jnp.where(low, across_x, encoded[0])], axis=0)
+    next_x = lax.ppermute(pair, "xl", across)
+    local = attention(place, source_len, *given, 8, inner, 2, 2, local)
+    next_x, local = lax.optimization_barrier((next_x, local))
+    pair = jnp.concatenate([pair, next_x], axis=0)
+    z_shifts = (0, 2, 1, 3)
+    along_z = [pair] + [lax.ppermute(pair, "z", ring(s)) for s in z_shifts[1:]]
+    local = attention(place, source_len, *given, 8, inner, 4, 4, local)
     moved = lax.all_to_all(local, ("xl", "z"), split_axis=0, concat_axis=0, tiled=True)
 
-    near, key_send, value_send, _ = lax.optimization_barrier((near, key_weight, value_weight, local))
+    near = jnp.concatenate(along_z, axis=0)
+    key_send, value_send, _ = lax.optimization_barrier((key_weight, value_weight, local))
     shifts = (0, 2, 1, 3)
     own_rows = [near] + [lax.ppermute(near, "y", ring(s)) for s in shifts[1:]]
     other_kw = lax.ppermute(key_send, "c", across)
@@ -288,10 +306,10 @@
         partial, ("xl", "z", "y", "xh"), split_axis=0, concat_axis=0, tiled=True
     )
 
-    spot = lax.axis_index("y").astype(jnp.int32).reshape(1)
+    spot = jnp.stack([lax.axis_index(a).astype(jnp.int32) for a in ("xl", "z", "y")])
     by_y = (8, 4, 2 * block, 4 * inner)
     key_update, value_update = updates(
-        spot, shifts, own_rows + other_rows, moved.reshape(by_y), other_moved.reshape(by_y), inner
+        spot, z_shifts, shifts, own_rows + other_rows, moved.reshape(by_y), other_moved.reshape(by_y), inner
     )
     encoder_grad = jnp.sum(terms.reshape(64, block, width).astype(F32), axis=0)
     return encoder_grad[None], key_update[None], value_update[None]

time: 108 us -> 108 us (level)
  waiting for transfers between devices: 35.8 us -> 29.7 us
  Pallas kernels: 40.7 us -> 46.2 us
  local copies, waits for them, and re-layouts: 2.5 us -> 0.9 us
  starting transfers between devices: 27 us -> 28.2 us
    ppermute x0 -> x5, starting transfers between devices: none -> 9.8 us  [the longest x3 5.96 us: body(): along_z = [pair] + [lax.ppermute(pair, 'z', ring(s)) for s in z_shifts[1:]]]
    all_to_all x1 -> x0, starting transfers between devices: 7.96 us -> none  [body(): lax.all_to_all(spread, ('xl', 'z', 'xh'), split_axis=0, concat_axis=0, ti...]
    all_to_all x1 -> x0, waiting for transfers between devices: 5.37 us -> none  [body(): lax.all_to_all(spread, ('xl', 'z', 'xh'), split_axis=0, concat_axis=0, ti...]
    pallas_call x1 -> x3, Pallas kernels: 6.92 us -> 11.8 us  [attention(): pl.pallas_call(attention_kernel, grid_spec=pltpu.PrefetchScalarGridSpec(n...]
    broadcast_in_dim x1 -> x0, local copies, waits for them, and re-layouts: 1.66 us -> none  [body(): spread = jnp.broadcast_to(encoded, (16, block, width))]
  transfers between devices with their start and end apart: 13 -> 17, of which waited for: 9 -> 9; matrix products, arithmetic and copies ran while one was open for 0% -> 1% of each run, Pallas kernels for 38% -> 43%
where the time goes in v3:
time: 108 us
  Pallas kernels  46.2 us (43%)
  waiting for transfers between devices  29.7 us (28%)
  starting transfers between devices  28.2 us (26%)
  other arithmetic  1.65 us (2%)
    pallas_call x1, Pallas kernels, updates(): pl.pallas_call(functools.partial(update_kernel, z_shifts, y_shifts), grid...  23.7 us
    ppermute x3, waiting for transfers between devices, body(): own_rows = [near] + [lax.ppermute(near, 'y', ring(s)) for s in shifts[1:]]  16.9 us
    pallas_call x3, Pallas kernels, attention(): pl.pallas_call(attention_kernel, grid_spec=pltpu.PrefetchScalarGridSpec(n...  11.8 us
    pallas_call x1, Pallas kernels, encoder_partial(): pl.pallas_call(partial_kernel, grid=(width // tile,), in_specs=[pl.BlockS...  10.7 us
    ppermute x3, starting transfers between devices, body(): own_rows = [near] + [lax.ppermute(near, 'y', ring(s)) for s in shifts[1:]]  6.24 us
    all_to_all x1, starting transfers between devices, body(): lax.all_to_all(partial, ('xl', 'z', 'y', 'xh'), split_axis=0, concat_axis...  6.13 us
    ppermute x3, starting transfers between devices, body(): along_z = [pair] + [lax.ppermute(pair, 'z', ring(s)) for s in z_shifts[1:]]  5.96 us
    all_to_all x1, waiting for transfers between devices, body(): lax.all_to_all(partial, ('xl', 'z', 'y', 'xh'), split_axis=0, concat_axis...  5.76 us
  transfers between devices with their start and end apart: 17, of which 9 were waited for; matrix products, arithmetic and copies ran while one was open for 1% of the time, Pallas kernels for 43%

profile of v3, /device:TPU:0, one launch (start us, length us, event | category | flops | bytes accessed | tf_op | source)
XLA Modules:
  0.0 107.5 jit_solution(16188975866733490675)
XLA Ops:
  0.6 3.2 %collective-permute-start = (bf16[8,2560]{1,0:T(8,128)(2,1)}, bf16[8,2560]{1,0:T(8,128)(2,1)S(1)}, u32[]{:S(2)}, u32[]{:S(2)}) collective-permute-start(bf16[8,2560]{1,0:T(8,128)(2,1)} %bitcast.35), channel_id=1, source_target_pairs={{0,1},{1,0},{2,3},{3,2},{4,5},{5,4},{6,7},{7,6},{8,9},{9,8},{10,11... | collective-permute-start | bytes 122888 | tf_op jit(solution)/shard_map/ppermute | solution.py:279
  3.8 3.7 %attention.3.refs_0_ = bf16[8,64,2048]{2,1,0:T(8,128)(2,1)} custom-call(s32[1]{0:T(128)} %bitcast.place, s32[16]{0:T(128)} %lens.5, bf16[128,8192]{1,0:T(8,128)(2,1)} %bitcast.22, bf16[64,8192]{1,0:T(8,128)(2,1)} %bitcast.28, bf16[64,8192]{1,0:T(8,128)(2,1)} %bitcast.31, bf16[128,8192]{1,0:T(8,128)(2,1)} %bitcast.25), custom_call_target="tpu_custom_call" | custom-call | flops 350000000 | bytes 4194304 | tf_op jit(solution)/shard_map/attention/pallas_call | solution.py:69
  7.6 0.0 collective-permute-done
  7.6 0.7 collective-permute-start.1
  8.3 3.6 %attention.4.refs_0_ = bf16[8,64,2048]{2,1,0:T(8,128)(2,1)} custom-call(s32[1]{0:T(128)} %bitcast.place, s32[16]{0:T(128)} %lens.5, bf16[128,8192]{1,0:T(8,128)(2,1)} %bitcast.23, bf16[64,8192]{1,0:T(8,128)(2,1)} %bitcast.29, bf16[64,8192]{1,0:T(8,128)(2,1)} %bitcast.32, bf16[128,8192]{1,0:T(8,128)(2,1)} %bitcast.26, ...), custom_call_target="tpu_custom_call", output_to_operand_aliasing={{}: (6, {})} | custom-call | flops 350000000 | bytes 4194304 | tf_op jit(solution)/shard_map/attention/pallas_call | solution.py:69
  11.9 0.3 collective-permute-done.1
  12.2 4.1 %collective-permute-start.4 = (bf16[32,2560]{1,0:T(8,128)(2,1)S(1)}, bf16[32,2560]{1,0:T(8,128)(2,1)S(1)}, u32[]{:S(2)}, u32[]{:S(2)}) collective-permute-start(bf16[32,2560]{1,0:T(8,128)(2,1)S(1)} %pad_maximum_fusion), channel_id=1, source_target_pairs={{0,48},{16,0},{32,16},{48,32},{1,49},{17,1},{33,17},{49,33},{2,50}... | collective-permute-start | bytes 491528 | tf_op jit(solution)/shard_map/ppermute | solution.py:289
  16.3 1.9 %collective-permute-start.2 = (bf16[32,2560]{1,0:T(8,128)(2,1)S(1)}, bf16[32,2560]{1,0:T(8,128)(2,1)S(1)}, u32[]{:S(2)}, u32[]{:S(2)}) collective-permute-start(bf16[32,2560]{1,0:T(8,128)(2,1)S(1)} %pad_maximum_fusion), channel_id=1, source_target_pairs={{0,32},{16,48},{32,0},{48,16},{1,33},{17,49},{33,1},{49,17},{2,34}... | collective-permute-start | bytes 491528 | tf_op jit(solution)/shard_map/ppermute | solution.py:289
  18.1 4.5 %attention.5 = bf16[8,64,2048]{2,1,0:T(8,128)(2,1)} custom-call(s32[1]{0:T(128)} %bitcast.place, s32[16]{0:T(128)} %lens.5, bf16[128,8192]{1,0:T(8,128)(2,1)} %bitcast.24, bf16[64,8192]{1,0:T(8,128)(2,1)} %bitcast.30, bf16[64,8192]{1,0:T(8,128)(2,1)} %bitcast.33, bf16[128,8192]{1,0:T(8,128)(2,1)} %bitcast.27, ...), custom_call_target="tpu_custom_call", output_to_operand_aliasing={{}: (6, {})} | custom-call | flops 350000000 | bytes 4194304 | tf_op jit(solution)/shard_map/attention/pallas_call | solution.py:69
  22.6 4.4 %all-to-all-start = ((bf16[8,64,2048]{2,1,0:T(8,128)(2,1)}), bf16[8,64,2048]{2,1,0:T(8,128)(2,1)}, u32[]{:S(2)}, u32[]{:S(2)}) async-start(bf16[8,64,2048]{2,1,0:T(8,128)(2,1)} %attention.5), calls=%async_computation | async-start | bytes 4194304 | tf_op jit(solution)/shard_map/all_to_all | solution.py:291
  27.0 0.1 collective-permute-start.7
  27.1 0.5 collective-permute-start.8
  27.7 3.1 %collective-permute-start.6 = (bf16[128,2560]{1,0:T(8,128)(2,1)S(1)}, bf16[128,2560]{1,0:T(8,128)(2,1)S(1)}, u32[]{:S(2)}, u32[]{:S(2)}) collective-permute-start(bf16[128,2560]{1,0:T(8,128)(2,1)S(1)} %constant_dynamic-update-slice_fusion.refs_0_), channel_id=1, source_target_pairs={{0,6},{2,0},{4,2},{6,4},{1,7},{3,1},{5,3},{7,5},{8,14},{10,8},{12,... | collective-permute-start | bytes 1966088 | tf_op jit(solution)/shard_map/ppermute | solution.py:296
  30.7 14.2 %collective-permute-done.6.refs_3_ = bf16[128,2560]{1,0:T(8,128)(2,1)S(1)} collective-permute-done((bf16[128,2560]{1,0:T(8,128)(2,1)S(1)}, bf16[128,2560]{1,0:T(8,128)(2,1)S(1)}, u32[]{:S(2)}, u32[]{:S(2)}) %collective-permute-start.6) | collective-permute-done | bytes 655392 | tf_op jit(solution)/shard_map/ppermute | solution.py:296
  45.0 0.8 copy-done.2
  45.8 2.7 %collective-permute-done.5.refs_2_ = bf16[128,2560]{1,0:T(8,128)(2,1)} collective-permute-done((bf16[128,2560]{1,0:T(8,128)(2,1)S(1)}, bf16[128,2560]{1,0:T(8,128)(2,1)}, u32[]{:S(2)}, u32[]{:S(2)}) %collective-permute-start.5) | collective-permute-done | bytes 655392 | tf_op jit(solution)/shard_map/ppermute | solution.py:296
  48.5 3.1 %all-to-all-done = bf16[8,64,2048]{2,1,0:T(8,128)(2,1)} async-done(((bf16[8,64,2048]{2,1,0:T(8,128)(2,1)}), bf16[8,64,2048]{2,1,0:T(8,128)(2,1)}, u32[]{:S(2)}, u32[]{:S(2)}) %all-to-all-start) | async-done | bytes 2097184 | tf_op jit(solution)/shard_map/all_to_all | solution.py:291
  51.6 3.2 %collective-permute-start.9 = (bf16[128,2560]{1,0:T(8,128)(2,1)S(1)}, bf16[128,2560]{1,0:T(8,128)(2,1)}, u32[]{:S(2)}, u32[]{:S(2)}) collective-permute-start(bf16[128,2560]{1,0:T(8,128)(2,1)S(1)} %constant_dynamic-update-slice_fusion.refs_0_), channel_id=1, source_target_pairs={{0,4},{2,6},{4,0},{6,2},{1,5},{3,7},{5,1},{7,3},{8,12},{10,14},{12... | collective-permute-start | bytes 1966088 | tf_op jit(solution)/shard_map/ppermute | solution.py:296
  54.8 10.7 %encoder_partial.1 = bf16[512,2560]{1,0:T(8,128)(2,1)} custom-call(bf16[512,2048]{1,0:T(8,128)(2,1)} %bitcast.6.kv_ref, bf16[2560,512]{1,0:T(8,128)(2,1)} %bitcast.38, bf16[2560,512]{1,0:T(8,128)(2,1)} %bitcast.40, bf16[2560,512]{1,0:T(8,128)(2,1)} %collective-permute-done.7.okw_ref, bf16[2560,512]{1,0:T(8,128)(2,1)} %collective-permute-done.8.ovw_ref), custom_call_target="tpu_custom_call" | custom-call | flops 5368709120 | bytes 16777216 | tf_op jit(solution)/shard_map/encoder_partial/pallas_call | solution.py:105
  65.5 6.1 %all-to-all-start.1 = ((bf16[64,8,2560]{2,1,0:T(8,128)(2,1)}), bf16[64,8,2560]{2,1,0:T(8,128)(2,1)S(1)}, u32[]{:S(2)}, u32[]{:S(2)}) async-start(bf16[64,8,2560]{2,1,0:T(8,128)(2,1)} %bitcast.34), calls=%async_computation.1 | async-start | bytes 5242880 | tf_op jit(solution)/shard_map/all_to_all | solution.py:305
  71.7 0.1 collective-permute-start.10
  71.8 0.5 collective-permute-start.11
  72.3 0.1 collective-permute-start.12
  72.4 0.4 collective-permute-start.13
  72.8 0.6 pad_add_fusion.spot
  73.4 0.6 collective-permute-done.10.refs_4_
  74.0 1.1 %collective-permute-done.11.refs_5_ = bf16[128,2560]{1,0:T(8,128)(2,1)} collective-permute-done((bf16[128,2560]{1,0:T(8,128)(2,1)}, bf16[128,2560]{1,0:T(8,128)(2,1)}, u32[]{:S(2)}, u32[]{:S(2)}) %collective-permute-start.11) | collective-permute-done | bytes 655392 | tf_op jit(solution)/shard_map/ppermute | solution.py:302
  75.1 0.9 collective-permute-done.12.refs_6_
  76.1 0.9 collective-permute-done.13.refs_7_
  77.0 23.7 %updates.1 = (f32[2560,512]{1,0:T(8,128)}, f32[2560,512]{1,0:T(8,128)}) custom-call(s32[3]{0:T(128)} %pad_add_fusion.spot, bf16[128,2560]{1,0:T(8,128)(2,1)} %copy-done.1, bf16[128,2560]{1,0:T(8,128)(2,1)} %collective-permute-done.9.refs_1_, bf16[128,2560]{1,0:T(8,128)(2,1)} %collective-permute-done.5.refs_2_, bf16[128,2560]{1,0:T(8,128)(2,1)} %copy-done.2, ...), custom_call_target="tpu_custom_call" | custom-call | flops 20000000000 | bytes 20971520 | tf_op jit(solution)/shard_map/updates/pallas_call | solution.py:240
  100.8 5.8 %all-to-all-done.1 = bf16[64,8,2560]{2,1,0:T(8,128)(2,1)S(1)} async-done(((bf16[64,8,2560]{2,1,0:T(8,128)(2,1)}), bf16[64,8,2560]{2,1,0:T(8,128)(2,1)S(1)}, u32[]{:S(2)}, u32[]{:S(2)}) %all-to-all-start.1) | async-done | bytes 2621472 | tf_op jit(solution)/shard_map/all_to_all | solution.py:305
  106.5 1.0 convert_reduce_fusion
  (23 shorter events, 0.1 us)
Async XLA Ops:
  0.6 6.9 %collective-permute-start = (bf16[8,2560]{1,0:T(8,128)(2,1)}, bf16[8,2560]{1,0:T(8,128)(2,1)S(1)}, u32[]{:S(2)}, u32[]{:S(2)}) collective-permute-start(bf16[8,2560]{1,0:T(8,128)(2,1)} %bitcast.35), channel_id=1, source_target_pairs={{0,1},{1,0},{2,3},{3,2},{4,5},{5,4},{6,7},{7,6},{8,9},{9,8},{10,11... | collective-permute-start | bytes 122888 | tf_op jit(solution)/shard_map/ppermute | solution.py:279
  3.8 3.8 %copy-start = (bf16[1,8,2560]{2,1,0:T(8,128)(2,1)S(1)}, bf16[1,8,2560]{2,1,0:T(8,128)(2,1)}, u32[]{:S(2)}) copy-start(bf16[1,8,2560]{2,1,0:T(8,128)(2,1)} %param.8) | copy-start | bytes 122884
  7.6 4.5 %collective-permute-start.1 = (bf16[16,2560]{1,0:T(8,128)(2,1)S(1)}, bf16[16,2560]{1,0:T(8,128)(2,1)S(1)}, u32[]{:S(2)}, u32[]{:S(2)}) collective-permute-start(bf16[16,2560]{1,0:T(8,128)(2,1)S(1)} %pad_maximum_fusion.1), channel_id=1, source_target_pairs={{0,64},{64,0},{1,65},{65,1},{2,66},{66,2},{3,67},{67,3},{4,68},{68... | collective-permute-start | bytes 245768 | tf_op jit(solution)/shard_map/ppermute | solution.py:284
  12.2 15.5 %collective-permute-start.4 = (bf16[32,2560]{1,0:T(8,128)(2,1)S(1)}, bf16[32,2560]{1,0:T(8,128)(2,1)S(1)}, u32[]{:S(2)}, u32[]{:S(2)}) collective-permute-start(bf16[32,2560]{1,0:T(8,128)(2,1)S(1)} %pad_maximum_fusion), channel_id=1, source_target_pairs={{0,48},{16,0},{32,16},{48,32},{1,49},{17,1},{33,17},{49,33},{2,50}... | collective-permute-start | bytes 491528 | tf_op jit(solution)/shard_map/ppermute | solution.py:289
  16.2 11.4 %collective-permute-start.3 = (bf16[32,2560]{1,0:T(8,128)(2,1)S(1)}, bf16[32,2560]{1,0:T(8,128)(2,1)S(1)}, u32[]{:S(2)}, u32[]{:S(2)}) collective-permute-start(bf16[32,2560]{1,0:T(8,128)(2,1)S(1)} %pad_maximum_fusion), channel_id=1, source_target_pairs={{0,16},{16,32},{32,48},{48,0},{1,17},{17,33},{33,49},{49,1},{2,18}... | collective-permute-start | bytes 491528 | tf_op jit(solution)/shard_map/ppermute | solution.py:289
  16.3 11.3 %collective-permute-start.2 = (bf16[32,2560]{1,0:T(8,128)(2,1)S(1)}, bf16[32,2560]{1,0:T(8,128)(2,1)S(1)}, u32[]{:S(2)}, u32[]{:S(2)}) collective-permute-start(bf16[32,2560]{1,0:T(8,128)(2,1)S(1)} %pad_maximum_fusion), channel_id=1, source_target_pairs={{0,32},{16,48},{32,0},{48,16},{1,33},{17,49},{33,1},{49,17},{2,34}... | collective-permute-start | bytes 491528 | tf_op jit(solution)/shard_map/ppermute | solution.py:289
  22.6 29.1 %all-to-all-start = ((bf16[8,64,2048]{2,1,0:T(8,128)(2,1)}), bf16[8,64,2048]{2,1,0:T(8,128)(2,1)}, u32[]{:S(2)}, u32[]{:S(2)}) async-start(bf16[8,64,2048]{2,1,0:T(8,128)(2,1)} %attention.5), calls=%async_computation | async-start | bytes 4194304 | tf_op jit(solution)/shard_map/all_to_all | solution.py:291
  27.0 27.8 %collective-permute-start.7 = (bf16[2560,512]{1,0:T(8,128)(2,1)}, bf16[2560,512]{1,0:T(8,128)(2,1)}, u32[]{:S(2)}, u32[]{:S(2)}) collective-permute-start(bf16[2560,512]{1,0:T(8,128)(2,1)} %bitcast.37), channel_id=1, source_target_pairs={{0,8},{8,0},{1,9},{9,1},{2,10},{10,2},{3,11},{11,3},{4,12},{12,4},... | collective-permute-start | bytes 7864328 | tf_op jit(solution)/shard_map/ppermute | solution.py:297
  27.1 27.7 %collective-permute-start.8 = (bf16[2560,512]{1,0:T(8,128)(2,1)}, bf16[2560,512]{1,0:T(8,128)(2,1)}, u32[]{:S(2)}, u32[]{:S(2)}) collective-permute-start(bf16[2560,512]{1,0:T(8,128)(2,1)} %bitcast.39), channel_id=1, source_target_pairs={{0,8},{8,0},{1,9},{9,1},{2,10},{10,2},{3,11},{11,3},{4,12},{12,4},... | collective-permute-start | bytes 7864328 | tf_op jit(solution)/shard_map/ppermute | solution.py:298
  27.7 44.0 %copy-start.1 = (bf16[128,2560]{1,0:T(8,128)(2,1)}, bf16[128,2560]{1,0:T(8,128)(2,1)S(1)}, u32[]{:S(2)}) copy-start(bf16[128,2560]{1,0:T(8,128)(2,1)S(1)} %constant_dynamic-update-slice_fusion.refs_0_) | copy-start | bytes 1966084
  27.7 17.3 %collective-permute-start.6 = (bf16[128,2560]{1,0:T(8,128)(2,1)S(1)}, bf16[128,2560]{1,0:T(8,128)(2,1)S(1)}, u32[]{:S(2)}, u32[]{:S(2)}) collective-permute-start(bf16[128,2560]{1,0:T(8,128)(2,1)S(1)} %constant_dynamic-update-slice_fusion.refs_0_), channel_id=1, source_target_pairs={{0,6},{2,0},{4,2},{6,4},{1,7},{3,1},{5,3},{7,5},{8,14},{10,8},{12,... | collective-permute-start | bytes 1966088 | tf_op jit(solution)/shard_map/ppermute | solution.py:296
  30.7 17.8 %collective-permute-start.5 = (bf16[128,2560]{1,0:T(8,128)(2,1)S(1)}, bf16[128,2560]{1,0:T(8,128)(2,1)}, u32[]{:S(2)}, u32[]{:S(2)}) collective-permute-start(bf16[128,2560]{1,0:T(8,128)(2,1)S(1)} %constant_dynamic-update-slice_fusion.refs_0_), channel_id=1, source_target_pairs={{0,2},{2,4},{4,6},{6,0},{1,3},{3,5},{5,7},{7,1},{8,10},{10,12},{12... | collective-permute-start | bytes 1966088 | tf_op jit(solution)/shard_map/ppermute | solution.py:296
  45.0 0.8 copy-start.2
  51.6 25.4 %collective-permute-start.14 = (bf16[8,64,2048]{2,1,0:T(8,128)(2,1)}, bf16[8,64,2048]{2,1,0:T(8,128)(2,1)}, u32[]{:S(2)}, u32[]{:S(2)}) collective-permute-start(bf16[8,64,2048]{2,1,0:T(8,128)(2,1)} %all-to-all-done), channel_id=1, source_target_pairs={{0,8},{8,0},{1,9},{9,1},{2,10},{10,2},{3,11},{11,3},{4,12},{12,4},... | collective-permute-start | bytes 6291464 | tf_op jit(solution)/shard_map/ppermute | solution.py:303
  51.6 20.1 %collective-permute-start.9 = (bf16[128,2560]{1,0:T(8,128)(2,1)S(1)}, bf16[128,2560]{1,0:T(8,128)(2,1)}, u32[]{:S(2)}, u32[]{:S(2)}) collective-permute-start(bf16[128,2560]{1,0:T(8,128)(2,1)S(1)} %constant_dynamic-update-slice_fusion.refs_0_), channel_id=1, source_target_pairs={{0,4},{2,6},{4,0},{6,2},{1,5},{3,7},{5,1},{7,3},{8,12},{10,14},{12... | collective-permute-start | bytes 1966088 | tf_op jit(solution)/shard_map/ppermute | solution.py:296
  65.5 41.0 %all-to-all-start.1 = ((bf16[64,8,2560]{2,1,0:T(8,128)(2,1)}), bf16[64,8,2560]{2,1,0:T(8,128)(2,1)S(1)}, u32[]{:S(2)}, u32[]{:S(2)}) async-start(bf16[64,8,2560]{2,1,0:T(8,128)(2,1)} %bitcast.34), calls=%async_computation.1 | async-start | bytes 5242880 | tf_op jit(solution)/shard_map/all_to_all | solution.py:305
  71.7 2.3 %collective-permute-start.10 = (bf16[128,2560]{1,0:T(8,128)(2,1)S(1)}, bf16[128,2560]{1,0:T(8,128)(2,1)}, u32[]{:S(2)}, u32[]{:S(2)}) collective-permute-start(bf16[128,2560]{1,0:T(8,128)(2,1)S(1)} %constant_dynamic-update-slice_fusion.refs_0_), channel_id=1, source_target_pairs={{0,8},{8,0},{1,9},{9,1},{2,10},{10,2},{3,11},{11,3},{4,12},{12,4},... | collective-permute-start | bytes 1966088 | tf_op jit(solution)/shard_map/ppermute | solution.py:302
  71.8 3.4 %collective-permute-start.11 = (bf16[128,2560]{1,0:T(8,128)(2,1)}, bf16[128,2560]{1,0:T(8,128)(2,1)}, u32[]{:S(2)}, u32[]{:S(2)}) collective-permute-start(bf16[128,2560]{1,0:T(8,128)(2,1)} %collective-permute-done.9.refs_1_), channel_id=1, source_target_pairs={{0,8},{8,0},{1,9},{9,1},{2,10},{10,2},{3,11},{11,3},{4,12},{12,4},... | collective-permute-start | bytes 1966088 | tf_op jit(solution)/shard_map/ppermute | solution.py:302
  72.3 3.8 %collective-permute-start.12 = (bf16[128,2560]{1,0:T(8,128)(2,1)}, bf16[128,2560]{1,0:T(8,128)(2,1)}, u32[]{:S(2)}, u32[]{:S(2)}) collective-permute-start(bf16[128,2560]{1,0:T(8,128)(2,1)} %collective-permute-done.5.refs_2_), channel_id=1, source_target_pairs={{0,8},{8,0},{1,9},{9,1},{2,10},{10,2},{3,11},{11,3},{4,12},{12,4},... | collective-permute-start | bytes 1966088 | tf_op jit(solution)/shard_map/ppermute | solution.py:302
  72.4 4.6 %collective-permute-start.13 = (bf16[128,2560]{1,0:T(8,128)(2,1)}, bf16[128,2560]{1,0:T(8,128)(2,1)}, u32[]{:S(2)}, u32[]{:S(2)}) collective-permute-start(bf16[128,2560]{1,0:T(8,128)(2,1)} %copy-done.2), channel_id=1, source_target_pairs={{0,8},{8,0},{1,9},{9,1},{2,10},{10,2},{3,11},{11,3},{4,12},{12,4},... | collective-permute-start | bytes 1966088 | tf_op jit(solution)/shard_map/ppermute | solution.py:302
